TPU v7x, 128 devices: a whole 4x4x4 slice. The times are simulated.
128 devices in a mesh: clu: 128 (over x, z, y, core).
Axes of the slice: x: 4, y: 4, z: 4, core: 2. Of those that a mesh axis runs over, the one named last changes fastest.
Arguments:
- charges: bfloat16 [1024, 32, 256], P('clu'), may hold values from -6 to 6
- basis: bfloat16 [1024, 96, 256], P('clu'), may hold values from -0.375 to 0.375
- transfer: bfloat16 [1024, 96, 96], P('clu'), may hold values from -0.4375 to 0.4375
- near_field: bfloat16 [1024, 3, 256, 256], P('clu'), may hold values from -0.21875 to 0.21875
- coupling: bfloat16 [16384, 96, 96], P('clu'), may hold values from -0.625 to 0.625
- ranks: int32 [1536], P('clu'), may hold values from 32 to 96, as said below
- block_source: int32 [16384], P('clu'), may hold values from 0 to 1535, as said below
- block_target: int32 [16384], P('clu'), may hold values from 0 to 1535, as said below
Outputs:
- first: bfloat16 [1024, 32, 256], P('clu')
- second: bfloat16 [1024, 32, 256], P('clu')
Inputs may be any that keep to these rules, and one draw needn't show every extreme that they name: `ranks`: each cluster's rank; 96 and 32 are both taken. `block_source`: global cluster numbers; a block's source and target are both leaves or both parents. Among the blocks of one device, at most 2 have their source on any one device, and exactly 2 for some device. `block_target`: global cluster numbers of the same level as the block's source. Among the blocks of one device, at most 2 have their target on any one device, and exactly 2 for some device.
All inputs are finite; a program needn't handle non-finite values.
Results may differ from a plain program's by a relative error of at most 0.025.
Values may be sent and summed in bfloat16 or wider, within the bound.
A program may use at most 128 MiB of HBM per device.

v0:
```python
import jax
import jax.numpy as jnp
from jax import lax
from jax.sharding import PartitionSpec as P


def with_halo(cells, sides, width):
    for axis, dim in sides:
        count = lax.axis_size(axis)
        ends = count - 1
        head = lax.slice_in_dim(cells, 0, width, axis=dim)
        tail = lax.slice_in_dim(cells, cells.shape[dim] - width, cells.shape[dim], axis=dim)
        cells = jnp.concatenate(
            [
                lax.ppermute(tail, axis, [(i, (i + 1) % count) for i in range(ends)]),
                cells,
                lax.ppermute(head, axis, [((i + 1) % count, i) for i in range(ends)]),
            ],
            axis=dim,
        )
    return cells


def slot_ranking(devices):
    same = devices[:, None] == devices[None, :]
    positions = jnp.arange(devices.shape[0])
    earlier = positions[None, :] < positions[:, None]
    return jnp.sum((same & earlier).astype(jnp.int32), axis=1)


def local(charges, basis, transfer, near_field, coupling, ranks, block_source, block_target):
    leaves = basis.shape[0]
    rank_top = basis.shape[1]
    right_sides = charges.shape[1]
    clusters = ranks.shape[0]
    blocks = coupling.shape[0]
    devices_all = lax.axis_size("clu")
    per_peer = max(2, 2 * blocks // devices_all)
    slot_rows = per_peer * devices_all
    flat = right_sides * rank_top
    rank_mask = (jnp.arange(rank_top)[None, :] < ranks[:, None]).astype(jnp.float32)
    leaf_mask = rank_mask[:leaves][:, None, :]
    parent_mask = rank_mask[leaves:][:, None, :]
    target_dev = block_target // clusters
    back_rows = target_dev * per_peer + slot_ranking(target_dev)
    unused = jnp.full((slot_rows,), -1, jnp.int32)
    wanted_targets = unused.at[back_rows].set(block_target % clusters)
    owner_ids = lax.all_to_all(wanted_targets, "clu", split_axis=0, concat_axis=0, tiled=True)
    selector = (owner_ids[None, :] == jnp.arange(clusters)[:, None]).astype(jnp.float32)
    pairs = transfer.reshape(leaves // 2, 2, rank_top, rank_top)

    def pick_rows(piece):
        valid = (block_source >= 0) & (block_source < piece.shape[0])
        rows_now = piece[jnp.clip(block_source, 0, piece.shape[0] - 1)]
        return jnp.where(valid[:, None], rows_now, jnp.zeros_like(rows_now))

    def apply_matrix(field_in):
        leaf_coeff = jnp.einsum("irb,ikb->irk", field_in, basis, preferred_element_type=jnp.float32)
        leaf_coeff = (leaf_coeff * leaf_mask).astype(jnp.bfloat16)
        kids = leaf_coeff.reshape(leaves // 2, 2, right_sides, rank_top)
        parent_coeff = jnp.einsum("qcrk,qckp->qrp", kids, pairs, preferred_element_type=jnp.float32)
        parent_coeff = (parent_coeff * parent_mask).astype(jnp.bfloat16)
        coeffs = jnp.concatenate([leaf_coeff, parent_coeff], axis=0).reshape(clusters, flat)
        sources = pick_rows(lax.all_gather(coeffs, "clu", axis=0, tiled=True))
        terms = jnp.einsum(
            "jrk,jkp->jrp",
            sources.reshape(blocks, right_sides, rank_top),
            coupling,
            preferred_element_type=jnp.float32,
        ).reshape(blocks, flat)
        outbound = jnp.zeros((slot_rows, flat), jnp.float32).at[back_rows].set(terms)
        returned = lax.all_to_all(
            outbound.astype(jnp.bfloat16), "clu", split_axis=0, concat_axis=0, tiled=True
        ).astype(outbound.dtype)
        padded = with_halo(field_in, (("clu", 0),), 1)
        near_sum = jnp.einsum(
            "irb,iba->ira", padded[0:leaves], near_field[:, 0], preferred_element_type=jnp.float32
        )
        for offset in range(1, 3):
            near_sum = near_sum + jnp.einsum(
                "irb,iba->ira",
                padded[offset : offset + leaves],
                near_field[:, offset],
                preferred_element_type=jnp.float32,
            )
        summed = jnp.dot(
            selector, returned, precision=lax.Precision.HIGHEST, preferred_element_type=jnp.float32
        )
        field = (summed.reshape(clusters, right_sides, rank_top) * rank_mask[:, None, :]).astype(
            jnp.bfloat16
        )
        downward = jnp.einsum(
            "qrp,qckp->qcrk", field[leaves:], pairs, preferred_element_type=jnp.float32
        )
        leaf_total = field[:leaves].astype(jnp.float32) + downward.reshape(
            leaves, right_sides, rank_top
        )
        leaf_total = (leaf_total * leaf_mask).astype(jnp.bfloat16)
        far_sum = jnp.einsum("irk,ikb->irb", leaf_total, basis, preferred_element_type=jnp.float32)
        return (near_sum + far_sum).astype(jnp.bfloat16)

    first = apply_matrix(charges)
    second = apply_matrix(first)
    return (first, second)


def solution(mesh):
    in_specs = (
        P("clu", None, None),
        P("clu", None, None),
        P("clu", None, None),
        P("clu", None, None, None),
        P("clu", None, None),
        P("clu"),
        P("clu"),
        P("clu"),
    )
    out_specs = (P("clu", None, None), P("clu", None, None))
    return jax.shard_map(local, mesh=mesh, in_specs=in_specs, out_specs=out_specs, check_vma=False)
```

profile of v0, /device:TPU:1, one launch (start us, length us, event | category | flops | bytes accessed | tf_op | source)
XLA Modules:
  0.0 346.7 jit_solution(3743502111903446637)
XLA Ops:
  14.0 12.0 %all-to-all-start = ((s32[128,2,1]{1,2,0:T(1,128)}), s32[128,2,1]{1,2,0:T(1,128)}, u32[]{:S(2)}, u32[]{:S(2)}) async-start(s32[128,2,1]{1,2,0:T(1,128)} %bitcast.3), calls=%async_computation | async-start | bytes 131072 | tf_op jit(solution)/shard_map/all_to_all | solution.py:48
  26.0 3.5 %copy.58 = bf16[128,96,96]{2,1,0:T(8,128)(2,1)S(1)} copy(bf16[128,96,96]{0,2,1:T(8,128)(2,1)} %param.12) | data formatting | bytes 4718592 | tf_op args[4]
  32.0 56.7 %all-gather.5.cloned.1.call-done = bf16[128,12,3072]{2,1,0:T(8,128)(2,1)} async-done(((bf16[1,12,3072]{2,1,0:T(8,128)(2,1)}), bf16[128,12,3072]{2,1,0:T(8,128)(2,1)}) %all-gather.5.cloned.1.call-update) | async-done | bytes 9437200 | tf_op jit(solution)/shard_map/all_gather | solution.py:64
  88.7 13.7 %reshape.133 = bf16[1536,3072]{1,0:T(8,128)(2,1)} reshape(bf16[128,12,3072]{2,1,0:T(8,128)(2,1)} %all-gather.5.cloned.1.call-done) | data formatting | bytes 18874368
  102.4 7.7 %gather_fusion = bf16[128,3072]{1,0:T(8,128)(2,1)} fusion(bf16[1536,3072]{1,0:T(8,128)(2,1)} %reshape.133, s32[1024]{0:T(1024)} %pad_clamp_fusion), kind=kCustom, calls=%fused_computation | custom fusion | bytes 1573376 | tf_op jit(solution)/shard_map/gather | solution.py:54
  110.1 2.3 copy.56
  114.5 2.7 copy.57
  117.2 3.5 %fusion.69 = f32[128,32,96]{2,1,0:T(8,128)} fusion(bf16[128,32,96]{2,1,0:T(8,128)(2,1)} %copy.57, bf16[128,96,96]{2,1,0:T(8,128)(2,1)S(1)} %copy.58), kind=kOutput, calls=%fused_computation.98 | convolution fusion | flops 75497472 | bytes 4718592 | tf_op jit(solution)/shard_map/jrk,jkp->jrp/dot_general | solution.py:65
  120.7 2.9 copy.59
  123.6 3.0 copy.60
  126.6 4.2 %scatter_custom_fusion.1 = f32[256,3072]{1,0:T(8,128)} fusion(s32[128]{0:T(128)} %copy-done.10, f32[128,3072]{1,0:T(8,128)} %copy.60, f32[]{:T(128)} %constant.31.clone.1), kind=kCustom, calls=%fused_computation.7 | custom fusion | bytes 3146240 | tf_op jit(solution)/shard_map/scatter | solution.py:71
  130.8 3.3 convert_element_type.59
  134.1 4.5 %all_to_all.24 = bf16[128,2,3072]{2,1,0:T(2,128)(2,1)} reshape(bf16[256,3072]{1,0:T(8,128)(2,1)} %convert_element_type.59) | data formatting | bytes 3145728 | tf_op jit(solution)/shard_map/all_to_all | solution.py:72
  138.5 7.8 %all-to-all-start.1 = ((bf16[128,2,3072]{2,1,0:T(2,128)(2,1)}), bf16[128,2,3072]{2,1,0:T(2,128)(2,1)}, u32[]{:S(2)}, u32[]{:S(2)}) async-start(bf16[128,2,3072]{2,1,0:T(2,128)(2,1)} %all_to_all.24), calls=%async_computation.1 | async-start | bytes 3145728 | tf_op jit(solution)/shard_map/all_to_all | solution.py:72
  147.7 3.0 collective-permute-start.1
  150.7 2.7 collective-permute-start
  163.8 6.9 %all-to-all-done.1 = bf16[128,2,3072]{2,1,0:T(2,128)(2,1)} async-done(((bf16[128,2,3072]{2,1,0:T(2,128)(2,1)}), bf16[128,2,3072]{2,1,0:T(2,128)(2,1)}, u32[]{:S(2)}, u32[]{:S(2)}) %all-to-all-start.1) | async-done | bytes 1572896 | tf_op jit(solution)/shard_map/all_to_all | solution.py:72
  170.7 4.6 %all_to_all.26 = bf16[256,3072]{1,0:T(8,128)(2,1)} reshape(bf16[128,2,3072]{2,1,0:T(2,128)(2,1)} %all-to-all-done.1) | data formatting | bytes 3145728 | tf_op jit(solution)/shard_map/all_to_all | solution.py:72
  175.3 2.6 copy.61
  186.1 71.3 %all-gather.7.cloned.1.call-done = bf16[128,12,3072]{2,1,0:T(8,128)(2,1)} async-done(((bf16[1,12,3072]{2,1,0:T(8,128)(2,1)}), bf16[128,12,3072]{2,1,0:T(8,128)(2,1)}) %all-gather.7.cloned.1.call-update) | async-done | bytes 9437200 | tf_op jit(solution)/shard_map/all_gather | solution.py:64
  257.4 13.7 %reshape.135 = bf16[1536,3072]{1,0:T(8,128)(2,1)} reshape(bf16[128,12,3072]{2,1,0:T(8,128)(2,1)} %all-gather.7.cloned.1.call-done) | data formatting | bytes 18874368
  271.1 7.7 %gather_fusion.1 = bf16[128,3072]{1,0:T(8,128)(2,1)} fusion(bf16[1536,3072]{1,0:T(8,128)(2,1)} %reshape.135, s32[1024]{0:T(1024)} %pad_clamp_fusion), kind=kCustom, calls=%fused_computation.1 | custom fusion | bytes 1573376 | tf_op jit(solution)/shard_map/gather | solution.py:54
  278.8 2.3 copy.63
  283.2 2.7 copy.64
  285.9 3.5 %fusion.71 = f32[128,32,96]{2,1,0:T(8,128)} fusion(bf16[128,32,96]{2,1,0:T(8,128)(2,1)} %copy.64, bf16[128,96,96]{2,1,0:T(8,128)(2,1)S(1)} %copy.58), kind=kOutput, calls=%fused_computation.100 | convolution fusion | flops 75497472 | bytes 4718592 | tf_op jit(solution)/shard_map/jrk,jkp->jrp/dot_general | solution.py:65
  293.1 3.1 scatter_custom_fusion.2
  297.6 4.5 %all_to_all.27 = bf16[128,2,3072]{2,1,0:T(2,128)(2,1)} reshape(bf16[256,3072]{1,0:T(8,128)(2,1)} %convert_element_type.66) | data formatting | bytes 3145728 | tf_op jit(solution)/shard_map/all_to_all | solution.py:72
  302.1 7.4 %all-to-all-start.2 = ((bf16[128,2,3072]{2,1,0:T(2,128)(2,1)}), bf16[128,2,3072]{2,1,0:T(2,128)(2,1)S(1)}, u32[]{:S(2)}, u32[]{:S(2)}) async-start(bf16[128,2,3072]{2,1,0:T(2,128)(2,1)} %all_to_all.27), calls=%async_computation.2 | async-start | bytes 3145728 | tf_op jit(solution)/shard_map/all_to_all | solution.py:72
  310.1 3.0 collective-permute-start.3
  315.3 2.6 collective-permute-start.2
  317.9 7.1 %collective-permute-done.3 = bf16[1,32,256]{2,1,0:T(8,128)(2,1)S(1)} collective-permute-done((bf16[1,32,256]{2,1,0:T(8,128)(2,1)S(1)}, bf16[1,32,256]{2,1,0:T(8,128)(2,1)S(1)}, u32[]{:S(2)}, u32[]{:S(2)}) %collective-permute-start.3) | collective-permute-done | bytes 16416 | tf_op jit(solution)/shard_map/ppermute | solution.py:17
  327.2 6.9 %all-to-all-done.2 = bf16[128,2,3072]{2,1,0:T(2,128)(2,1)S(1)} async-done(((bf16[128,2,3072]{2,1,0:T(2,128)(2,1)}), bf16[128,2,3072]{2,1,0:T(2,128)(2,1)S(1)}, u32[]{:S(2)}, u32[]{:S(2)}) %all-to-all-start.2) | async-done | bytes 1572896 | tf_op jit(solution)/shard_map/all_to_all | solution.py:72
  (81 shorter events, 48.9 us)
Async XLA Ops:
  7.2 1.0 copy-start
  7.2 81.6 %all-gather.5.cloned.1.call-start = ((), (), s32[]{:S(2)}) async-start(), calls=%async_computation.3 | async-start | bytes 12681216 | tf_op jit(solution)/shard_map/all_gather | solution.py:64
  12.2 1.8 copy-start.10
  14.0 124.5 %all-to-all-start = ((s32[128,2,1]{1,2,0:T(1,128)}), s32[128,2,1]{1,2,0:T(1,128)}, u32[]{:S(2)}, u32[]{:S(2)}) async-start(s32[128,2,1]{1,2,0:T(1,128)} %bitcast.3), calls=%async_computation | async-start | bytes 131072 | tf_op jit(solution)/shard_map/all_to_all | solution.py:48
  138.5 32.2 %all-to-all-start.1 = ((bf16[128,2,3072]{2,1,0:T(2,128)(2,1)}), bf16[128,2,3072]{2,1,0:T(2,128)(2,1)}, u32[]{:S(2)}, u32[]{:S(2)}) async-start(bf16[128,2,3072]{2,1,0:T(2,128)(2,1)} %all_to_all.24), calls=%async_computation.1 | async-start | bytes 3145728 | tf_op jit(solution)/shard_map/all_to_all | solution.py:72
  146.3 111.1 %all-gather.7.cloned.1.call-start = ((), (), s32[]{:S(2)}) async-start(), calls=%async_computation.4 | async-start | bytes 12681216 | tf_op jit(solution)/shard_map/all_gather | solution.py:64
  147.7 13.9 %collective-permute-start.1 = (bf16[1,32,256]{2,1,0:T(8,128)(2,1)}, bf16[1,32,256]{2,1,0:T(8,128)(2,1)}, u32[]{:S(2)}, u32[]{:S(2)}) collective-permute-start(bf16[1,32,256]{2,1,0:T(8,128)(2,1)} %get-tuple-element.5), channel_id=1, source_target_pairs={{1,0},{2,1},{3,2},{4,3},{5,4},{6,5},{7,6},{8,7},{9,8},{10,9},{11,1... | collective-permute-start | bytes 49160 | tf_op jit(solution)/shard_map/ppermute | solution.py:17
  150.7 30.7 %collective-permute-start = (bf16[1,32,256]{2,1,0:T(8,128)(2,1)}, bf16[1,32,256]{2,1,0:T(8,128)(2,1)}, u32[]{:S(2)}, u32[]{:S(2)}) collective-permute-start(bf16[1,32,256]{2,1,0:T(8,128)(2,1)} %get-tuple-element.4), channel_id=1, source_target_pairs={{0,1},{1,2},{2,3},{3,4},{4,5},{5,6},{6,7},{7,8},{8,9},{9,10},{10,1... | collective-permute-start | bytes 49160 | tf_op jit(solution)/shard_map/ppermute | solution.py:15
  177.9 3.6 %copy-start.2 = (bf16[8,32,256]{2,1,0:T(8,128)(2,1)S(1)}, bf16[8,32,256]{2,1,0:T(8,128)(2,1)}, u32[]{:S(2)}) copy-start(bf16[8,32,256]{2,1,0:T(8,128)(2,1)} %param.8) | copy-start | bytes 393220
  177.9 3.6 %copy-start.6 = (f32[8,32,256]{2,1,0:T(8,128)S(1)}, f32[8,32,256]{2,1,0:T(8,128)}, u32[]{:S(2)}) copy-start(f32[8,32,256]{2,1,0:T(8,128)} %fusion.22) | copy-start | bytes 786436
  177.9 3.6 %copy-start.12 = (f32[8,32,256]{2,1,0:T(8,128)S(1)}, f32[8,32,256]{2,1,0:T(8,128)}, u32[]{:S(2)}) copy-start(f32[8,32,256]{2,1,0:T(8,128)} %fusion.18) | copy-start | bytes 786436
  177.9 5.4 %copy-start.1 = (bf16[8,96,96]{2,1,0:T(8,128)(2,1)S(1)}, bf16[8,96,96]{2,1,0:T(8,128)(2,1)}, u32[]{:S(2)}) copy-start(bf16[8,96,96]{2,1,0:T(8,128)(2,1)} %param.10) | copy-start | bytes 442372
  183.1 0.7 copy-start.3
  271.1 10.1 %copy-start.9 = (pred[128]{0:T(512)(128)(4,1)S(1)}, pred[128]{0:T(512)(128)(4,1)}, u32[]{:S(2)}) copy-start(pred[128]{0:T(512)(128)(4,1)} %compare_and_fusion) | copy-start | bytes 388
  297.6 11.9 %copy-start.4 = (bf16[8,32,256]{2,1,0:T(8,128)(2,1)S(1)}, bf16[8,32,256]{2,1,0:T(8,128)(2,1)}, u32[]{:S(2)}) copy-start(bf16[8,32,256]{2,1,0:T(8,128)(2,1)} %copy-done.3) | copy-start | bytes 393220
  302.1 32.1 %all-to-all-start.2 = ((bf16[128,2,3072]{2,1,0:T(2,128)(2,1)}), bf16[128,2,3072]{2,1,0:T(2,128)(2,1)S(1)}, u32[]{:S(2)}, u32[]{:S(2)}) async-start(bf16[128,2,3072]{2,1,0:T(2,128)(2,1)} %all_to_all.27), calls=%async_computation.2 | async-start | bytes 3145728 | tf_op jit(solution)/shard_map/all_to_all | solution.py:72
  310.1 14.9 %collective-permute-start.3 = (bf16[1,32,256]{2,1,0:T(8,128)(2,1)S(1)}, bf16[1,32,256]{2,1,0:T(8,128)(2,1)S(1)}, u32[]{:S(2)}, u32[]{:S(2)}) collective-permute-start(bf16[1,32,256]{2,1,0:T(8,128)(2,1)S(1)} %get-tuple-element.3), channel_id=1, source_target_pairs={{1,0},{2,1},{3,2},{4,3},{5,4},{6,5},{7,6},{8,7},{9,8},{10,9},{11,1... | collective-permute-start | bytes 49160 | tf_op jit(solution)/shard_map/ppermute | solution.py:17
  315.3 22.3 %collective-permute-start.2 = (bf16[1,32,256]{2,1,0:T(8,128)(2,1)}, bf16[1,32,256]{2,1,0:T(8,128)(2,1)}, u32[]{:S(2)}, u32[]{:S(2)}) collective-permute-start(bf16[1,32,256]{2,1,0:T(8,128)(2,1)} %get-tuple-element.2), channel_id=1, source_target_pairs={{0,1},{1,2},{2,3},{3,4},{4,5},{5,6},{6,7},{7,8},{8,9},{9,10},{10,1... | collective-permute-start | bytes 49160 | tf_op jit(solution)/shard_map/ppermute | solution.py:15
  327.2 8.3 %copy-start.8 = (s32[256]{0:T(256)S(1)}, s32[256]{0:T(256)}, u32[]{:S(2)}) copy-start(s32[256]{0:T(256)} %eq.33) | copy-start | bytes 3076
  335.5 2.1 copy-start.5
  335.5 2.1 copy-start.7
  335.5 2.1 copy-start.11
Sparse Core Ops, SparseCore 0:
  11.7 77.0 all-gather.4
  186.2 71.1 all-gather.6
where the time goes:
time: 349 us; the launch traced here: 347 us
  waiting for transfers between devices  151 us (43%)
  local copies, waits for them, and re-layouts  99.4 us (28%)
  starting transfers between devices  38.4 us (11%)
  matrix products  27.7 us (8%)
  other arithmetic  16 us (5%)
  between operations  14.4 us (4%)
    all_gather x2, waiting for transfers between devices, apply_matrix(): sources = pick_rows(lax.all_gather(coeffs, 'clu', axis=0, tiled=True))  128 us
    unnamed x31, local copies, waits for them, and re-layouts  33.8 us
    gather x4, local copies, waits for them, and re-layouts, pick_rows(): rows_now = piece[jnp.clip(block_source, 0, piece.shape[0] - 1)]  20.1 us
    all_to_all x2, starting transfers between devices, apply_matrix(): lax.all_to_all(outbound.astype(jnp.bfloat16), 'clu', split_axis=0, concat...  15.1 us
    all_to_all x4, local copies, waits for them, and re-layouts, apply_matrix(): lax.all_to_all(outbound.astype(jnp.bfloat16), 'clu', split_axis=0, concat...  14.2 us
    all_to_all x2, waiting for transfers between devices, apply_matrix(): lax.all_to_all(outbound.astype(jnp.bfloat16), 'clu', split_axis=0, concat...  13.8 us
    all_to_all x1, starting transfers between devices, local(): lax.all_to_all(wanted_targets, 'clu', split_axis=0, concat_axis=0, tiled=...  12 us
    dot_general x4, matrix products, apply_matrix(): jnp.einsum('irb,iba->ira', padded[offset:offset + leaves], near_field[:,...  9 us
  transfers between devices with their start and end apart: 9, of which 6 were waited for; matrix products, arithmetic and copies ran while one was open for 22% of the time, Pallas kernels for 0%

commit v1 on v0

v1 whole, which is shorter than its diff:
```python
import jax
import jax.numpy as jnp
from jax import lax
from jax.experimental import pallas as pl
from jax.experimental.pallas import tpu as pltpu
from jax.sharding import PartitionSpec as P

MESH = pl.DeviceIdType.MESH
F32 = jnp.float32
BF16 = jnp.bfloat16
RMAX = 96
RHS = 32
LEAF = 256
STRIDE = {"x": 32, "z": 8, "y": 2}
ROUTES = (("y", "x", "z"), ("z", "y", "x"), ("x", "z", "y"))
WIDE = 1024
HALF = WIDE // 2
GROUPS = 8
SLOTS = 32
BLOCKS = 128

G1, G2, EX0, EX1, R2, R1 = 0, 4, 8, 17, 26, 30
PER_ROUTE = 34
HALO = 3 * PER_ROUTE
COPIES = HALO + 2


def dot(a, b):
    return jnp.dot(a, b, preferred_element_type=F32)


def dot_nt(a, b):
    return lax.dot_general(a, b, (((1,), (1,)), ((), ())), preferred_element_type=F32)


def kernel(
    charges, basis, transfer, near_hbm, coupling_hbm, mask, lists, source_slot, target_slot,
    out,
    near, coupling, v, near_sum, lists_in, pick, scatter, unpick, place,
    small, big_in, big_out, products, gathered, outbox, inbox, passing,
    total, partial, half_out, half_in, full_out, full_in,
    half1_out, half1_in, full1_out, full1_in,
    send_sem, recv_sem, list_send, list_recv, load_sem,
):
    me = lax.axis_index("clu")
    devices = 128
    core = lax.rem(me, 2)
    pos = {a: lax.rem(lax.div(me, s), 4) for a, s in STRIDE.items()}

    def at(axis, step):
        return lax.rem(pos[axis] + (step + 4), 4)

    def near_by(axis, step, other=0):
        base = me + (at(axis, step) - pos[axis]) * STRIDE[axis]
        return base + (1 - 2 * core) if other else base

    sibling = me + (1 - 2 * core)
    before = lax.rem(me + devices - 1, devices)
    after = lax.rem(me + 1, devices)

    barrier = pltpu.get_barrier_semaphore()
    peers = [sibling, before, after]
    for axis in STRIDE:
        for step in (1, -1, 2):
            for other in (0, 1):
                peers.append(near_by(axis, step, other))
    for peer in peers:
        pl.semaphore_signal(barrier, inc=1, device_id=(peer,), device_id_type=MESH)

    load_near = pltpu.make_async_copy(near_hbm, near, load_sem.at[0])
    load_coupling = pltpu.make_async_copy(coupling_hbm, coupling, load_sem.at[1])
    load_near.start()
    load_coupling.start()
    v[0, 1:9] = charges[...]
    small[...] = jnp.zeros_like(small)

    lane = lax.broadcasted_iota(jnp.int32, (16, 128), 1)

    def merge(row, extra, u, width):
        lanes = lax.broadcasted_iota(jnp.int32, (width, 128), 1)
        return jnp.where(lanes < RMAX, row, pltpu.roll(extra, RMAX - 32 * u, 1))

    def fourth(parts, width):
        lanes = lax.broadcasted_iota(jnp.int32, (width, 128), 1)
        rolled = [pltpu.roll(part, 32 + 32 * u, 1) for u, part in enumerate(parts)]
        return jnp.where(lanes < 32, rolled[0], jnp.where(lanes < 64, rolled[1], rolled[2]))

    def coefficients(p):
        for q in range(4):
            total_q = jnp.zeros((RHS, RMAX), F32)
            for i in (2 * q, 2 * q + 1):
                c = dot_nt(v[p, 1 + i], basis[i]) * mask[i : i + 1, :RMAX]
                c = c.astype(BF16)
                small[pl.ds(i, RHS, stride=16), 0:RMAX] = c.astype(F32)
                total_q = total_q + dot(c, transfer[i])
            c = (total_q * mask[8 + q : 9 + q, :RMAX]).astype(BF16)
            small[pl.ds(8 + q, RHS, stride=16), 0:RMAX] = c.astype(F32)
        for u, (first, second, _) in enumerate(ROUTES):
            where = pos[second] * 4 + pos[first]
            for g in range(8):
                row = small[(4 * g + u) * 16 : (4 * g + u + 1) * 16, :]
                extra = small[(4 * g + 3) * 16 : (4 * g + 4) * 16, :]
                gathered[p, u, where, :, g * 128 : (g + 1) * 128] = merge(row, extra, u, 16).astype(BF16)

    def near_part(p, lo, hi):
        def body(i, carry):
            s = dot(v[p, i], near[i, 0])
            s = s + dot(v[p, i + 1], near[i, 1])
            s = s + dot(v[p, i + 2], near[i, 2])
            near_sum[i] = s
            return carry

        lax.fori_loop(lo, hi, body, 0)

    list_copies = []
    for u, (_, _, axis) in enumerate(ROUTES):
        mine = pos[axis] * 2 + core
        targets = [(near_by(axis, s, o), at(axis, s) * 2 + (1 - core if o else core))
                   for s in (1, -1, 2) for o in (0, 1)]
        targets.append((sibling, pos[axis] * 2 + 1 - core))
        for k, (device, group) in enumerate(targets):
            list_copies.append(pltpu.make_async_remote_copy(
                src_ref=lists.at[u, group], dst_ref=lists_in.at[u, mine],
                send_sem=list_send.at[u * 7 + k], recv_sem=list_recv.at[u * 7 + k],
                device_id=(device,), device_id_type=MESH))

    def make_selectors():
        rows = lax.broadcasted_iota(jnp.int32, (256, 256), 0)
        for u, (_, _, axis) in enumerate(ROUTES):
            mine = pos[axis] * 2 + core
            lists_in[u, mine] = lists[u, mine]
            both = lists_in[u, 0]
            for q in range(1, 8):
                both = jnp.maximum(both, lists_in[u, q])
            hit = jnp.where(rows == both[0:1, :], 1.0, 0.0).astype(F32)
            pick[u] = jnp.transpose(hit, (1, 0)).astype(BF16)
            scatter[u] = jnp.where(rows == both[1:2, :], 1.0, 0.0).astype(BF16)
            lanes = lax.broadcasted_iota(jnp.int32, (128, 256), 1)
            unpick[u] = jnp.where(lanes == source_slot[:, u : u + 1], 1.0, 0.0).astype(BF16)
            slots = lax.broadcasted_iota(jnp.int32, (256, 128), 0)
            place[u] = jnp.where(slots == target_slot[u : u + 1, :], 1.0, 0.0).astype(BF16)

    coefficients(0)
    pl.semaphore_wait(barrier, len(peers))

    def product(p, carry):
        started = []

        def remote(k, src, dst, device):
            copy = pltpu.make_async_remote_copy(
                src_ref=src, dst_ref=dst, send_sem=send_sem.at[p, k], recv_sem=recv_sem.at[p, k],
                device_id=(device,), device_id_type=MESH)
            started.append(copy)
            copy.start()
            return copy

        halo = [
            remote(HALO, v.at[p, 1], v.at[p, 9], before),
            remote(HALO + 1, v.at[p, 8], v.at[p, 0], after),
        ]

        ring = []
        for u, (axis, second, _) in enumerate(ROUTES):
            base = u * PER_ROUTE + G1
            own = gathered.at[p, u, pos[second] * 4 + pos[axis]]
            ring.append((remote(base, own, own, near_by(axis, 1)), remote(base + 1, own, own, near_by(axis, -1))))

        @pl.when(p == 0)
        def _():
            for copy in list_copies:
                copy.start()

        later = []
        for u, (axis, second, _) in enumerate(ROUTES):
            base = u * PER_ROUTE + G1
            ring[u][0].wait_recv()
            left = gathered.at[p, u, pos[second] * 4 + at(axis, -1), :, pl.ds(0, HALF)]
            a = remote(base + 2, left, left, near_by(axis, 1))
            ring[u][1].wait_recv()
            right = gathered.at[p, u, pos[second] * 4 + at(axis, 1), :, pl.ds(HALF, HALF)]
            later.append((a, remote(base + 3, right, right, near_by(axis, -1))))

        ring = []
        for u, (_, axis, _) in enumerate(ROUTES):
            base = u * PER_ROUTE + G2
            later[u][0].wait_recv()
            later[u][1].wait_recv()
            own = gathered.at[p, u, pl.ds(pos[axis] * 4, 4)]
            ring.append((remote(base, own, own, near_by(axis, 1)), remote(base + 1, own, own, near_by(axis, -1))))

        @pl.when(p == 0)
        def _():
            for copy in list_copies:
                copy.wait()
            make_selectors()
            load_near.wait()
            load_coupling.wait()

        later = []
        for u, (_, axis, _) in enumerate(ROUTES):
            base = u * PER_ROUTE + G2
            ring[u][0].wait_recv()
            left = gathered.at[p, u, pl.ds(at(axis, -1) * 4, 2)]
            a = remote(base + 2, left, left, near_by(axis, 1))
            ring[u][1].wait_recv()
            right = gathered.at[p, u, pl.ds(at(axis, 1) * 4 + 2, 2)]
            later.append((a, remote(base + 3, right, right, near_by(axis, -1))))

        def exchange_start(way, u):
            axis = ROUTES[u][2]
            base = u * PER_ROUTE + (EX1 if way else EX0)
            box, to, via = outbox.at[p, way, u], inbox.at[p, way, u], passing.at[p, way, u]
            mine = to.at[pos[axis] * 2 + core]
            fwd = [remote(base + 4, box.at[at(axis, 2) * 2 + core], via.at[0], near_by(axis, 1)),
                   remote(base + 5, box.at[at(axis, 2) * 2 + 1 - core], via.at[1], near_by(axis, -1))]
            direct = []
            for s, step in enumerate((1, -1)):
                for o in (0, 1):
                    group = at(axis, step) * 2 + (1 - core if o else core)
                    direct.append(remote(base + 2 * s + o, box.at[group], mine, near_by(axis, step, o)))
            direct.append(remote(base + 8, box.at[pos[axis] * 2 + 1 - core], mine, sibling))
            inbox[p, way, u, pos[axis] * 2 + core] = outbox[p, way, u, pos[axis] * 2 + core]
            return fwd, direct

        def exchange_pass(way, u, fwd, direct):
            axis = ROUTES[u][2]
            base = u * PER_ROUTE + (EX1 if way else EX0)
            to, via = inbox.at[p, way, u], passing.at[p, way, u]
            fwd[0].wait_recv()
            direct.append(remote(base + 6, via.at[0], to.at[at(axis, -1) * 2 + core], near_by(axis, 1)))
            fwd[1].wait_recv()
            direct.append(remote(base + 7, via.at[1], to.at[at(axis, 1) * 2 + core], near_by(axis, -1, 1)))

        flight = []
        for u in range(3):
            later[u][0].wait_recv()
            later[u][1].wait_recv()

            def picks(n, carry, u=u):
                cols = pl.ds(pl.multiple_of(n * 256, 256), 256)
                rows = gathered[p, u, :, :, cols].reshape(256, 256)
                outbox[p, 0, u, :, :, cols] = dot(pick[u], rows).astype(BF16).reshape(GROUPS, SLOTS, 256)
                return carry

            lax.fori_loop(0, 4, picks, 0)
            flight.append(exchange_start(0, u))

        halo[0].wait_recv()
        halo[1].wait_recv()
        v[p, 0] = (v[p, 0].astype(F32) * (me > 0).astype(F32)).astype(BF16)
        v[p, 9] = (v[p, 9].astype(F32) * (me < devices - 1).astype(F32)).astype(BF16)
        near_part(p, 0, 2)
        for u in range(3):
            exchange_pass(0, u, *flight[u])
        near_part(p, 2, 6)
        for u in range(3):
            for copy in flight[u][1]:
                copy.wait_recv()

        def unpicks(n, carry):
            cols = pl.ds(pl.multiple_of(n * 256, 256), 256)
            parts = [dot(unpick[u], inbox[p, 0, u, :, :, cols].reshape(256, 256)) for u in range(3)]
            for k in range(2):
                g = 2 * n + k
                sides = [part[:, k * 128 : (k + 1) * 128] for part in parts]
                for u in range(3):
                    big_in[pl.ds(pl.multiple_of((4 * g + u) * 128, 128), 128), :] = sides[u]
                big_in[pl.ds(pl.multiple_of((4 * g + 3) * 128, 128), 128), :] = fourth(sides, 128)
            return carry

        lax.fori_loop(0, 4, unpicks, 0)

        def blocks(b, carry):
            for k in range(8):
                j = b * 8 + k
                x = big_in[pl.ds(j, RHS, stride=BLOCKS), 0:RMAX].astype(BF16)
                big_out[pl.ds(j, RHS, stride=BLOCKS), 0:RMAX] = dot(x, coupling[j])
            return carry

        lax.fori_loop(0, BLOCKS // 8, blocks, 0)

        def packs(g, carry):
            cols = pl.ds(pl.multiple_of(g * 128, 128), 128)
            extra = big_out[pl.ds(pl.multiple_of((4 * g + 3) * 128, 128), 128), :]
            for u in range(3):
                row = big_out[pl.ds(pl.multiple_of((4 * g + u) * 128, 128), 128), :]
                products[u, :, cols] = merge(row, extra, u, 128).astype(BF16)
            return carry

        lax.fori_loop(0, 8, packs, 0)

        flight = []
        for u in range(3):
            def places(n, carry, u=u):
                cols = pl.ds(pl.multiple_of(n * 256, 256), 256)
                sent = dot(place[u], products[u, :, cols]).astype(BF16)
                outbox[p, 1, u, :, :, cols] = sent.reshape(GROUPS, SLOTS, 256)
                return carry

            lax.fori_loop(0, 4, places, 0)
            flight.append(exchange_start(1, u))
        for u in range(3):
            exchange_pass(1, u, *flight[u])
        near_part(p, 6, 8)

        first_half = []
        for u, (_, axis, _) in enumerate(ROUTES):
            base = u * PER_ROUTE + R2
            for copy in flight[u][1]:
                copy.wait_recv()

            def sums(n, carry, u=u):
                cols = pl.ds(pl.multiple_of(n * 256, 256), 256)
                rows = inbox[p, 1, u, :, :, cols].reshape(256, 256)
                total[u, :, :, cols] = dot(scatter[u], rows).reshape(4, 64, 256)
                return carry

            lax.fori_loop(0, 4, sums, 0)
            far = at(axis, 2)
            half_out[p, u, 0] = total[u, far, :, 0:HALF].astype(BF16)
            half_out[p, u, 1] = total[u, far, :, HALF:WIDE].astype(BF16)
            first_half.append((
                remote(base, half_out.at[p, u, 0], half_in.at[p, u, 0], near_by(axis, 1)),
                remote(base + 1, half_out.at[p, u, 1], half_in.at[p, u, 1], near_by(axis, -1))))
        second_half = []
        for u, (_, axis, _) in enumerate(ROUTES):
            base = u * PER_ROUTE + R2
            up, down = at(axis, 1), at(axis, -1)
            first_half[u][0].wait_recv()
            full_out[p, u, 0, :, 0:HALF] = (total[u, up, :, 0:HALF] + half_in[p, u, 0].astype(F32)).astype(BF16)
            full_out[p, u, 0, :, HALF:WIDE] = total[u, up, :, HALF:WIDE].astype(BF16)
            a = remote(base + 2, full_out.at[p, u, 0], full_in.at[p, u, 0], near_by(axis, 1))
            first_half[u][1].wait_recv()
            full_out[p, u, 1, :, 0:HALF] = total[u, down, :, 0:HALF].astype(BF16)
            full_out[p, u, 1, :, HALF:WIDE] = (
                total[u, down, :, HALF:WIDE] + half_in[p, u, 1].astype(F32)).astype(BF16)
            second_half.append((a, remote(base + 3, full_out.at[p, u, 1], full_in.at[p, u, 1], near_by(axis, -1))))

        first_half = []
        for u, (axis, second, _) in enumerate(ROUTES):
            base = u * PER_ROUTE + R1
            second_half[u][0].wait_recv()
            second_half[u][1].wait_recv()
            for k in range(4):
                rows = slice(16 * k, 16 * k + 16)
                partial[u, k] = (total[u, pos[second], rows] + full_in[p, u, 0, rows].astype(F32)
                                 + full_in[p, u, 1, rows].astype(F32))
            far = at(axis, 2)
            half1_out[p, u, 0] = partial[u, far, :, 0:HALF].astype(BF16)
            half1_out[p, u, 1] = partial[u, far, :, HALF:WIDE].astype(BF16)
            first_half.append((
                remote(base, half1_out.at[p, u, 0], half1_in.at[p, u, 0], near_by(axis, 1)),
                remote(base + 1, half1_out.at[p, u, 1], half1_in.at[p, u, 1], near_by(axis, -1))))
        second_half = []
        for u, (axis, _, _) in enumerate(ROUTES):
            base = u * PER_ROUTE + R1
            up, down = at(axis, 1), at(axis, -1)
            first_half[u][0].wait_recv()
            full1_out[p, u, 0, :, 0:HALF] = (partial[u, up, :, 0:HALF] + half1_in[p, u, 0].astype(F32)).astype(BF16)
            full1_out[p, u, 0, :, HALF:WIDE] = partial[u, up, :, HALF:WIDE].astype(BF16)
            a = remote(base + 2, full1_out.at[p, u, 0], full1_in.at[p, u, 0], near_by(axis, 1))
            first_half[u][1].wait_recv()
            full1_out[p, u, 1, :, 0:HALF] = partial[u, down, :, 0:HALF].astype(BF16)
            full1_out[p, u, 1, :, HALF:WIDE] = (
                partial[u, down, :, HALF:WIDE] + half1_in[p, u, 1].astype(F32)).astype(BF16)
            second_half.append((a, remote(base + 3, full1_out.at[p, u, 1], full1_in.at[p, u, 1], near_by(axis, -1))))
        for u, (axis, _, _) in enumerate(ROUTES):
            second_half[u][0].wait_recv()
            second_half[u][1].wait_recv()
            partial[u, pos[axis]] = (partial[u, pos[axis]] + full1_in[p, u, 0].astype(F32)
                                     + full1_in[p, u, 1].astype(F32))
        for g in range(8):
            sides = [partial[u, pos[ROUTES[u][0]], :, g * 128 : (g + 1) * 128] for u in range(3)]
            for u in range(3):
                small[(4 * g + u) * 16 : (4 * g + u + 1) * 16, :] = sides[u]
            small[(4 * g + 3) * 16 : (4 * g + 4) * 16, :] = fourth(sides, 16)

        for q in range(4):
            above = (small[pl.ds(8 + q, RHS, stride=16), 0:RMAX] * mask[8 + q : 9 + q, :RMAX]).astype(BF16)
            for i in (2 * q, 2 * q + 1):
                own = mask[i : i + 1, :RMAX]
                here = (small[pl.ds(i, RHS, stride=16), 0:RMAX] * own).astype(BF16)
                leaf = ((here.astype(F32) + dot_nt(above, transfer[i])) * own).astype(BF16)
                result = (near_sum[i] + dot(leaf, basis[i])).astype(BF16)
                out[p, i] = result
                v[p + 1, 1 + i] = result

        @pl.when(p == 0)
        def _():
            small[...] = jnp.zeros_like(small)
            coefficients(p + 1)

        for copy in started:
            copy.wait_send()
        return carry

    lax.fori_loop(0, 2, product, 0)


def routing(clusters_of):
    device, local = clusters_of // 12, clusters_of % 12
    where = {a: (device // s) % 4 for a, s in STRIDE.items()}
    groups = jnp.stack([where[a] * 2 + device % 2 for _, _, a in ROUTES])
    rows = jnp.stack([where[b] * 64 + where[a] * 16 + local for a, b, _ in ROUTES])
    order = jnp.arange(BLOCKS)
    same = (groups[:, :, None] == groups[:, None, :]) & (order[None, None, :] < order[None, :, None])
    slot = groups * SLOTS + jnp.sum(same.astype(jnp.int32), axis=2)
    hit = slot[:, None, :] == jnp.arange(GROUPS * SLOTS)[None, :, None]
    wanted = jnp.max(jnp.where(hit, rows[:, None, :], -1), axis=2)
    return slot, wanted.reshape(3, GROUPS, SLOTS)


def local(charges, basis, transfer, near_field, coupling, ranks, block_source, block_target):
    me = lax.axis_index("clu")
    mask = (jnp.arange(128)[None, :] < jnp.pad(ranks, (0, 4))[:, None]).astype(F32)
    source_slot, source_rows = routing(block_source)
    target_slot, target_rows = routing(block_target)
    both = jnp.stack([source_rows, target_rows], axis=2)
    mine = jnp.stack([(me // STRIDE[a]) % 4 * 2 + me % 2 for _, _, a in ROUTES])
    spread = jnp.tile(both, (1, 1, 1, GROUPS))
    shown = (jnp.arange(GROUPS * SLOTS) // SLOTS)[None, :] == mine[:, None]
    lists = jnp.where(shown[:, None, None, :], spread, -1)
    lists = jnp.pad(lists, ((0, 0), (0, 0), (0, 6), (0, 0)), constant_values=-1)
    columns = jnp.pad(source_slot.T, ((0, 0), (0, 5)))
    lines = jnp.pad(target_slot, ((0, 5), (0, 0)))
    vmem = pl.BlockSpec(memory_space=pltpu.VMEM)
    hbm = pl.BlockSpec(memory_space=pl.ANY)
    both_out = pl.pallas_call(
        kernel,
        out_shape=jax.ShapeDtypeStruct((2, 8, RHS, LEAF), BF16),
        in_specs=[vmem, vmem, vmem, hbm, hbm, vmem, vmem, vmem, vmem],
        out_specs=vmem,
        scratch_shapes=[
            pltpu.VMEM((8, 3, LEAF, LEAF), BF16),
            pltpu.VMEM((BLOCKS, RMAX, RMAX), BF16),
            pltpu.VMEM((3, 10, RHS, LEAF), BF16),
            pltpu.VMEM((8, RHS, LEAF), F32),
            pltpu.VMEM((3, 8, 8, 256), jnp.int32),
            pltpu.VMEM((3, 256, 256), BF16),
            pltpu.VMEM((3, 256, 256), BF16),
            pltpu.VMEM((3, 128, 256), BF16),
            pltpu.VMEM((3, 256, 128), BF16),
            pltpu.VMEM((RHS * 16, 128), F32),
            pltpu.VMEM((RHS * BLOCKS, 128), F32),
            pltpu.VMEM((RHS * BLOCKS, 128), F32),
            pltpu.VMEM((3, BLOCKS, WIDE), BF16),
            pltpu.VMEM((2, 3, 16, 16, WIDE), BF16),
            pltpu.VMEM((2, 2, 3, GROUPS, SLOTS, WIDE), BF16),
            pltpu.VMEM((2, 2, 3, GROUPS, SLOTS, WIDE), BF16),
            pltpu.VMEM((2, 2, 3, 2, SLOTS, WIDE), BF16),
            pltpu.VMEM((3, 4, 64, WIDE), F32),
            pltpu.VMEM((3, 4, 16, WIDE), F32),
            pltpu.VMEM((2, 3, 2, 64, HALF), BF16),
            pltpu.VMEM((2, 3, 2, 64, HALF), BF16),
            pltpu.VMEM((2, 3, 2, 64, WIDE), BF16),
            pltpu.VMEM((2, 3, 2, 64, WIDE), BF16),
            pltpu.VMEM((2, 3, 2, 16, HALF), BF16),
            pltpu.VMEM((2, 3, 2, 16, HALF), BF16),
            pltpu.VMEM((2, 3, 2, 16, WIDE), BF16),
            pltpu.VMEM((2, 3, 2, 16, WIDE), BF16),
            pltpu.SemaphoreType.DMA((2, COPIES)),
            pltpu.SemaphoreType.DMA((2, COPIES)),
            pltpu.SemaphoreType.DMA((21,)),
            pltpu.SemaphoreType.DMA((21,)),
            pltpu.SemaphoreType.DMA((2,)),
        ],
        compiler_params=pltpu.CompilerParams(
            collective_id=0, has_side_effects=True, vmem_limit_bytes=56 * 1024 * 1024
        ),
    )(charges, basis, transfer, near_field, coupling, mask, lists, columns, lines)
    return both_out[0], both_out[1]


def solution(mesh):
    in_specs = (
        P("clu", None, None),
        P("clu", None, None),
        P("clu", None, None),
        P("clu", None, None, None),
        P("clu", None, None),
        P("clu"),
        P("clu"),
        P("clu"),
    )
    out_specs = (P("clu", None, None), P("clu", None, None))
    return jax.shard_map(local, mesh=mesh, in_specs=in_specs, out_specs=out_specs, check_vma=False)
```

time: 349 us -> 149 us (0.43)
  waiting for transfers between devices: 151 us -> 0 us
  Pallas kernels: 0 us -> 132 us
  local copies, waits for them, and re-layouts: 99.4 us -> 9.47 us
  starting transfers between devices: 38.4 us -> 0 us
  matrix products: 27.7 us -> 0 us
  between operations: 14.4 us -> 0.8 us
  other arithmetic: 16 us -> 5.07 us
    pallas_call x0 -> x1, Pallas kernels: none -> 132 us  [local(): pl.pallas_call(kernel, out_shape=jax.ShapeDtypeStruct((2, 8, RHS, LEAF),...]
    all_gather x2 -> x0, waiting for transfers between devices: 128 us -> none  [apply_matrix(): sources = pick_rows(lax.all_gather(coeffs, 'clu', axis=0, tiled=True))]
    unnamed x31 -> x2, local copies, waits for them, and re-layouts: 33.8 us -> 4.87 us
    dot_general x18 -> x0, matrix products: 27.7 us -> none  [the longest x4 9 us: apply_matrix(): jnp.einsum('irb,iba->ira', padded[offset:offset + leaves], near_field[:,...]
    all_to_all x3 -> x0, starting transfers between devices: 27.1 us -> none  [the longest x2 15.1 us: apply_matrix(): lax.all_to_all(outbound.astype(jnp.bfloat16), 'clu', split_axis=0, concat...]
    gather x4 -> x0, local copies, waits for them, and re-layouts: 20.1 us -> none  [pick_rows(): rows_now = piece[jnp.clip(block_source, 0, piece.shape[0] - 1)]]
    all_to_all x6 -> x0, local copies, waits for them, and re-layouts: 15.5 us -> none  [the longest x4 14.2 us: apply_matrix(): lax.all_to_all(outbound.astype(jnp.bfloat16), 'clu', split_axis=0, concat...]
    all_to_all x3 -> x0, waiting for transfers between devices: 13.8 us -> none  [the longest x2 13.8 us: apply_matrix(): lax.all_to_all(outbound.astype(jnp.bfloat16), 'clu', split_axis=0, concat...]
  transfers between devices with their start and end apart: 9 -> 0, of which waited for: 6 -> 0; matrix products, arithmetic and copies ran while one was open for 22% -> 0% of each run, Pallas kernels for 0% -> 0%
where the time goes in v1:
time: 149 us; the launch traced here: 147 us
  Pallas kernels  132 us (89%)
  local copies, waits for them, and re-layouts  9.47 us (6%)
  other arithmetic  5.07 us (3%)
    pallas_call x1, Pallas kernels, local(): pl.pallas_call(kernel, out_shape=jax.ShapeDtypeStruct((2, 8, RHS, LEAF),...  132 us
    unnamed x2, local copies, waits for them, and re-layouts  4.87 us

profile of v1, /device:TPU:1, one launch (start us, length us, event | category | flops | bytes accessed | tf_op | source)
XLA Modules:
  0.0 147.3 jit_solution(12777265969058764778)
XLA Ops:
  0.7 0.1 pad_add_fusion.5
  0.8 0.7 pad.16
  1.5 0.1 broadcast_compare_fusion
  1.5 0.7 add_bitcast_fusion.5
  2.2 0.7 add_bitcast_fusion.2
  2.9 0.7 add_bitcast_fusion.8
  3.6 0.7 add_bitcast_fusion.7
  4.3 0.7 add_bitcast_fusion.11
  5.0 0.7 fusion.mask
  5.7 0.3 convert_reduce_fusion.1
  6.0 0.2 select_reduce_fusion
  6.2 0.6 pad.19.target_slot
  6.9 0.2 select_reduce_fusion.1
  7.1 0.1 stack_reshape.6
  7.1 0.1 stack_reshape.7
  7.2 0.1 copy.15
  7.4 0.6 pad.18.clone.source_slot
  8.0 0.1 tile.10
  8.2 0.7 pad.17.lists
  8.9 4.8 %copy.13.coupling_hbm = bf16[128,96,96]{2,1,0:T(8,128)(2,1)} copy(bf16[128,96,96]{0,2,1:T(8,128)(2,1)} %param.12) | data formatting | bytes 4718592 | tf_op args[4]
  13.6 132.0 %shard_map.95 = bf16[2,8,32,256]{3,2,1,0:T(8,128)(2,1)} custom-call(bf16[8,32,256]{2,1,0:T(8,128)(2,1)} %charges.1, bf16[8,96,256]{2,1,0:T(8,128)(2,1)} %basis.1, bf16[8,96,96]{2,1,0:T(8,128)(2,1)} %transfer.1, bf16[8,3,256,256]{3,2,1,0:T(8,128)(2,1)} %near_hbm.1, bf16[128,96,96]{2,1,0:T(8,128)(2,1)} %copy.13.coupling_hbm, f32[16,128]{1,0:T(8,128)} %fusion.mask, ...), custom_call_target="tpu_custom_call" | custom-call | tf_op jit(solution)/shard_map/pallas_call | solution.py:428
  145.7 1.7 %slice_bitcast_fusion = (bf16[8,32,256]{2,1,0:T(8,128)(2,1)}, bf16[8,32,256]{2,1,0:T(8,128)(2,1)}) fusion(bf16[2,8,32,256]{3,2,1,0:T(8,128)(2,1)} %shard_map.95), kind=kLoop, calls=%fused_computation.6 | loop fusion | bytes 524288 | tf_op jit(solution)/shard_map/squeeze | solution.py:471
  (14 shorter events, 0.2 us)

commit v2 on v0

v2 whole, which is shorter than its diff:
```python
import jax
import jax.numpy as jnp
from jax import lax
from jax.experimental import pallas as pl
from jax.experimental.pallas import tpu as pltpu
from jax.sharding import PartitionSpec as P

MESH = pl.DeviceIdType.MESH
F32 = jnp.float32
BF16 = jnp.bfloat16
RMAX = 96
RHS = 32
PART = 16
LEAF = 256
STRIDE = {"x": 32, "z": 8, "y": 2}
ROUTES = (("y", "x", "z"), ("z", "y", "x"), ("x", "z", "y"))
STEPS = (2, 1, -1)
WIDE = 512
GROUPS = 8
SLOTS = 32
BLOCKS = 128

G1, G2, EX, R2, R1, HALO = 0, 9, 45, 87, 96, 105
COPIES = 107


def dot(a, b):
    return jnp.dot(a, b, preferred_element_type=F32)


def dot_nt(a, b):
    return lax.dot_general(a, b, (((1,), (1,)), ((), ())), preferred_element_type=F32)


def iota(shape, dim):
    return lax.broadcasted_iota(jnp.int32, shape, dim)


def ones_where(hit):
    return jnp.where(hit, 1.0, 0.0).astype(F32)


def merge(row, extra, u):
    return jnp.where(iota(row.shape, 1) < RMAX, row, pltpu.roll(extra, RMAX - 32 * u, 1))


def fourth(parts):
    rolled = [pltpu.roll(part, 32 + 32 * u, 1) for u, part in enumerate(parts)]
    lanes = iota(parts[0].shape, 1)
    return jnp.where(lanes < 32, rolled[0], jnp.where(lanes < 64, rolled[1], rolled[2]))


def kernel(
    charges, basis, transfer, near_hbm, coupling_hbm, ranks, block_source, block_target,
    first_out, second_out,
    near, turned, wide_coupling, coupling, v, near_sum, mask, raw, raw_in, meta, pick, scatter, unpick, place,
    small, big_in, big_out, products, gathered, outbox, inbox, sums_out, sums_in, ends_out, ends_in,
    send_sem, recv_sem, list_send, list_recv, load_sem,
):
    me = lax.axis_index("clu")
    devices = 128
    core = lax.rem(me, 2)
    pos = {a: lax.rem(lax.div(me, s), 4) for a, s in STRIDE.items()}

    def at(axis, step):
        return lax.rem(pos[axis] + (step + 4), 4)

    def near_by(axis, step, other=0):
        base = me + (at(axis, step) - pos[axis]) * STRIDE[axis]
        return base + (1 - 2 * core) if other else base

    sibling = me + (1 - 2 * core)
    before = lax.rem(me + devices - 1, devices)
    after = lax.rem(me + 1, devices)

    barrier = pltpu.get_barrier_semaphore()
    peers = [sibling, before, after]
    for axis in STRIDE:
        for step in STEPS:
            for other in (0, 1):
                peers.append(near_by(axis, step, other))
    for peer in peers:
        pl.semaphore_signal(barrier, inc=1, device_id=(peer,), device_id_type=MESH)

    load_near = pltpu.make_async_copy(near_hbm, near, load_sem.at[0])
    load_coupling = pltpu.make_async_copy(coupling_hbm, turned, load_sem.at[1])
    load_coupling.start()
    load_near.start()
    v[0, 1:9] = charges[...]
    small[...] = jnp.zeros_like(small)
    raw[...] = jnp.zeros_like(raw)
    raw[0:1, :] = block_source[...]
    raw[1:2, :] = block_target[...]
    for i in range(12):
        mask[i : i + 1, :] = ones_where(iota((1, 128), 1) < ranks[0:1, i : i + 1])

    def copy_of(p, h, k, src, dst, device):
        return pltpu.make_async_remote_copy(
            src_ref=src, dst_ref=dst, send_sem=send_sem.at[p, h, k], recv_sem=recv_sem.at[p, h, k],
            device_id=(device,), device_id_type=MESH)

    def coefficients(p, h):
        rows = pl.ds(PART * h, PART)
        for q in range(4):
            above = jnp.zeros((PART, RMAX), F32)
            for i in (2 * q, 2 * q + 1):
                c = dot_nt(v[p, 1 + i, rows], basis[i]) * mask[i : i + 1, :RMAX]
                c = c.astype(BF16)
                small[h, pl.ds(i, PART, stride=16), 0:RMAX] = c.astype(F32)
                above = above + dot(c, transfer[i])
            c = (above * mask[8 + q : 9 + q, :RMAX]).astype(BF16)
            small[h, pl.ds(8 + q, PART, stride=16), 0:RMAX] = c.astype(F32)
        for u, (first, second, _) in enumerate(ROUTES):
            where = pos[second] * 4 + pos[first]
            for g in range(4):
                row = small[h, (4 * g + u) * 16 : (4 * g + u + 1) * 16, :]
                extra = small[h, (4 * g + 3) * 16 : (4 * g + 4) * 16, :]
                gathered[p, h, u, where, :, g * 128 : (g + 1) * 128] = merge(row, extra, u).astype(BF16)

    def halo_copies(p, h):
        rows = pl.ds(PART * h, PART)
        return [
            copy_of(p, h, HALO, v.at[p, 1, rows], v.at[p, 9, rows], before),
            copy_of(p, h, HALO + 1, v.at[p, 8, rows], v.at[p, 0, rows], after),
        ]

    def first_gather(p, h):
        copies = []
        for u, (first, second, _) in enumerate(ROUTES):
            own = gathered.at[p, h, u, pos[second] * 4 + pos[first]]
            copies.append([copy_of(p, h, G1 + 3 * u + s, own, own, near_by(first, step))
                           for s, step in enumerate(STEPS)])
        return copies

    def second_gather(p, h, u, piece):
        first, second, _ = ROUTES[u]
        block = gathered.at[p, h, u, pos[second] * 4 + at(first, (0, -2, -1, 1)[piece])]
        return [copy_of(p, h, G2 + (4 * u + piece) * 3 + s, block, block, near_by(second, step))
                for s, step in enumerate(STEPS)]

    def begin(p, h):
        coefficients(p, h)
        for copies in first_gather(p, h):
            for copy in copies:
                copy.start()
        for u in range(3):
            for copy in second_gather(p, h, u, 0):
                copy.start()
        for copy in halo_copies(p, h):
            copy.start()

    def near_part(p, lo, hi):
        def body(i, carry):
            s = dot(v[p, i], near[i, 0])
            s = s + dot(v[p, i + 1], near[i, 1])
            near_sum[i] = s + dot(v[p, i + 2], near[i, 2])
            return carry

        lax.fori_loop(lo, hi, body, 0)

    list_copies = []
    for u, (_, _, axis) in enumerate(ROUTES):
        mine = pos[axis] * 2 + core
        targets = [near_by(axis, s, o) for s in STEPS for o in (0, 1)] + [sibling]
        for k, device in enumerate(targets):
            list_copies.append(pltpu.make_async_remote_copy(
                src_ref=raw, dst_ref=raw_in.at[u, pl.ds(pl.multiple_of(mine * 8, 8), 8)],
                send_sem=list_send.at[u * 7 + k], recv_sem=list_recv.at[u * 7 + k],
                device_id=(device,), device_id_type=MESH))

    def place_of(ids, route):
        first, second, axis = route
        device = lax.shift_right_logical(ids * 43691, 19)
        where = {a: lax.shift_right_logical(device, n) & 3 for a, n in (("x", 5), ("z", 3), ("y", 1))}
        group = where[axis] * 2 + (device & 1)
        return group, where[second] * 64 + where[first] * 16 + (ids - 12 * device)

    def make_selectors():
        ahead = ones_where(iota((128, 128), 0) < iota((128, 128), 1)).astype(BF16)
        for u, route in enumerate(ROUTES):
            axis = route[2]
            mine = pos[axis] * 2 + core
            group, _ = place_of(raw[...], route)
            slots = []
            for k in range(2):
                hit = ones_where(iota((8, 128), 0) == group[k : k + 1, :])
                rank = jnp.sum(hit * dot(hit.astype(BF16), ahead), axis=0, keepdims=True)
                slots.append(group[k : k + 1, :].astype(F32) * SLOTS + rank)
            number = iota((256, 128), 0).astype(F32)
            unpick[u] = jnp.transpose(ones_where(number == slots[0]), (1, 0)).astype(BF16)
            place[u] = ones_where(number == slots[1]).astype(BF16)
            raw_in[u, pl.ds(pl.multiple_of(mine * 8, 8), 8), :] = raw[...]
            for k in range(2):
                group, row = place_of(raw_in[u, pl.ds(k, 8, stride=8), :], route)
                hit = ones_where(group == mine)
                rank = dot(hit.astype(BF16), ahead)
                meta[k, 0] = jnp.where(group == mine, rank, -1.0)
                meta[k, 1] = row.astype(F32)

            def fill(q, carry, u=u):
                for k in range(2):
                    slot = ones_where(iota((SLOTS, 128), 0).astype(F32) == meta[k, 0, pl.ds(q, 1), :])
                    row = ones_where(iota((256, 128), 0).astype(F32) == meta[k, 1, pl.ds(q, 1), :])
                    lines = dot_nt(slot.astype(BF16), row.astype(BF16))
                    here = pl.ds(pl.multiple_of(q * SLOTS, SLOTS), SLOTS)
                    if k == 0:
                        pick[u, here, :] = lines.astype(BF16)
                    else:
                        big_in[0, here, :] = lines[:, 0:128]
                        big_in[1, here, :] = lines[:, 128:256]
                return carry

            lax.fori_loop(0, GROUPS, fill, 0)
            scatter[u, 0:128, :] = jnp.transpose(big_in[0, 0:256, :], (1, 0)).astype(BF16)
            scatter[u, 128:256, :] = jnp.transpose(big_in[1, 0:256, :], (1, 0)).astype(BF16)

    def turn(lo, hi):
        same = ones_where(iota((128, 128), 0) == iota((128, 128), 1)).astype(BF16)

        def body(n, carry):
            for k in range(4):
                row = 4 * n + k
                wide_coupling[pl.ds(row, BLOCKS, stride=RMAX), 0:RMAX] = dot_nt(same, turned[row])
            return carry

        lax.fori_loop(lo // 4, hi // 4, body, 0)

    def narrow():
        def body(n, carry):
            for k in range(4):
                j = 4 * n + k
                rows = pl.ds(pl.multiple_of(j * RMAX, RMAX), RMAX)
                coupling[j] = wide_coupling[rows, 0:RMAX].astype(BF16)
            return carry

        lax.fori_loop(0, BLOCKS // 4, body, 0)

    def exchange(p, h, way, u):
        axis = ROUTES[u][2]
        base = EX + 21 * way + 7 * u
        box = outbox.at[p, h, way, u]
        mine = inbox.at[p, h, way, u, pos[axis] * 2 + core]
        copies = []
        for s, step in enumerate(STEPS):
            for o in (0, 1):
                group = at(axis, step) * 2 + (1 - core if o else core)
                copies.append(copy_of(p, h, base + 2 * s + o, box.at[group], mine, near_by(axis, step, o)))
        copies.append(copy_of(p, h, base + 6, box.at[pos[axis] * 2 + 1 - core], mine, sibling))
        for copy in copies:
            copy.start()
        inbox[p, h, way, u, pos[axis] * 2 + core] = outbox[p, h, way, u, pos[axis] * 2 + core]
        return copies

    def tiles(body):
        lax.fori_loop(0, WIDE // 256, lambda n, carry: body(pl.ds(pl.multiple_of(n * 256, 256), 256), n), 0)

    def stream(p, h):
        started = []
        ring = first_gather(p, h)
        waits = []
        for u in range(3):
            waits.append(second_gather(p, h, u, 0))
        for s in range(3):
            for u in range(3):
                ring[u][s].wait_recv()
                copies = second_gather(p, h, u, 1 + s)
                for copy in copies:
                    copy.start()
                waits[u] += copies
        for u in range(3):
            started += ring[u] + waits[u]
        yield
        flight = []
        for u in range(3):
            for copy in waits[u]:
                copy.wait_recv()

            def picks(cols, n, u=u):
                rows = gathered[p, h, u, :, :, cols].reshape(256, 256)
                outbox[p, h, 0, u, :, :, cols] = dot(pick[u], rows).astype(BF16).reshape(GROUPS, SLOTS, 256)
                return 0

            tiles(picks)
            flight.append(exchange(p, h, 0, u))
        yield
        for u in range(3):
            started += flight[u]
            for copy in flight[u]:
                copy.wait_recv()

        def unpicks(cols, n):
            parts = [dot(unpick[u], inbox[p, h, 0, u, :, :, cols].reshape(256, 256)) for u in range(3)]
            for k in range(2):
                g = 2 * n + k
                sides = [part[:, k * 128 : (k + 1) * 128] for part in parts]
                for u in range(3):
                    big_in[h, pl.ds(pl.multiple_of((4 * g + u) * 128, 128), 128), :] = sides[u]
                big_in[h, pl.ds(pl.multiple_of((4 * g + 3) * 128, 128), 128), :] = fourth(sides)
            return 0

        tiles(unpicks)

        def blocks(b, carry):
            for k in range(16):
                j = b * 16 + k
                x = big_in[h, pl.ds(j, PART, stride=BLOCKS), 0:RMAX].astype(BF16)
                big_out[h, pl.ds(j, PART, stride=BLOCKS), 0:RMAX] = dot(x, coupling[j])
            return carry

        lax.fori_loop(0, BLOCKS // 16, blocks, 0)

        def packs(g, carry):
            cols = pl.ds(pl.multiple_of(g * 128, 128), 128)
            extra = big_out[h, pl.ds(pl.multiple_of((4 * g + 3) * 128, 128), 128), :]
            for u in range(3):
                row = big_out[h, pl.ds(pl.multiple_of((4 * g + u) * 128, 128), 128), :]
                products[h, u, :, cols] = merge(row, extra, u).astype(BF16)
            return carry

        lax.fori_loop(0, 4, packs, 0)
        flight = []
        for u in range(3):
            def places(cols, n, u=u):
                sent = dot(place[u], products[h, u, :, cols]).astype(BF16)
                outbox[p, h, 1, u, :, :, cols] = sent.reshape(GROUPS, SLOTS, 256)
                return 0

            tiles(places)
            flight.append(exchange(p, h, 1, u))
        yield
        parts = []
        for u, (_, axis, _) in enumerate(ROUTES):
            started += flight[u]
            for copy in flight[u]:
                copy.wait_recv()

            def sums(cols, n, u=u):
                rows = inbox[p, h, 1, u, :, :, cols].reshape(256, 256)
                sums_out[p, h, u, :, :, cols] = dot(scatter[u], rows).astype(BF16).reshape(4, 64, 256)
                return 0

            tiles(sums)
            copies = [copy_of(p, h, R2 + 3 * u + s, sums_out.at[p, h, u, at(axis, step)], sums_in.at[p, h, u, s],
                              near_by(axis, step)) for s, step in enumerate(STEPS)]
            for copy in copies:
                copy.start()
            parts.append(copies)
        yield
        ends = []
        for u, (axis, second, _) in enumerate(ROUTES):
            started += parts[u]
            for copy in parts[u]:
                copy.wait_recv()
            for k in range(4):
                rows = slice(16 * k, 16 * k + 16)
                s = sums_out[p, h, u, pos[second], rows].astype(F32)
                for n in range(3):
                    s = s + sums_in[p, h, u, n, rows].astype(F32)
                ends_out[p, h, u, k] = s.astype(BF16)
            copies = [copy_of(p, h, R1 + 3 * u + s, ends_out.at[p, h, u, at(axis, step)], ends_in.at[p, h, u, s],
                              near_by(axis, step)) for s, step in enumerate(STEPS)]
            for copy in copies:
                copy.start()
            ends.append(copies)
        yield
        sides = []
        for u, (axis, _, _) in enumerate(ROUTES):
            started += ends[u]
            for copy in ends[u]:
                copy.wait_recv()
            s = ends_out[p, h, u, pos[axis]].astype(F32)
            for n in range(3):
                s = s + ends_in[p, h, u, n].astype(F32)
            sides.append(s)
        for g in range(4):
            here = [s[:, g * 128 : (g + 1) * 128] for s in sides]
            for u in range(3):
                small[h, (4 * g + u) * 16 : (4 * g + u + 1) * 16, :] = here[u]
            small[h, (4 * g + 3) * 16 : (4 * g + 4) * 16, :] = fourth(here)
        lines = pl.ds(PART * h, PART)
        for q in range(4):
            above = (small[h, pl.ds(8 + q, PART, stride=16), 0:RMAX] * mask[8 + q : 9 + q, :RMAX]).astype(BF16)
            for i in (2 * q, 2 * q + 1):
                own = mask[i : i + 1, :RMAX]
                here = (small[h, pl.ds(i, PART, stride=16), 0:RMAX] * own).astype(BF16)
                leaf = ((here.astype(F32) + dot_nt(above, transfer[i])) * own).astype(BF16)
                v[p + 1, 1 + i, lines] = (near_sum[i, lines] + dot(leaf, basis[i])).astype(BF16)

        @pl.when(p == 0)
        def _():
            small[h] = jnp.zeros_like(small[h])
            begin(p + 1, h)

        for copy in started + halo_copies(p, h):
            copy.wait_send()
        yield

    pl.semaphore_wait(barrier, len(peers))
    begin(0, 0)
    begin(0, 1)
    for copy in list_copies:
        copy.start()

    def product(p, carry):
        streams = [stream(p, h) for h in (0, 1)]

        def both():
            for s in streams:
                next(s)

        both()

        @pl.when(p == 0)
        def _():
            for copy in list_copies:
                copy.wait()
            make_selectors()
            load_coupling.wait()
            turn(0, 32)
            load_near.wait()

        for h in (0, 1):
            for copy in halo_copies(p, h):
                copy.wait_recv()
        v[p, 0] = (v[p, 0].astype(F32) * (me > 0).astype(F32)).astype(BF16)
        v[p, 9] = (v[p, 9].astype(F32) * (me < devices - 1).astype(F32)).astype(BF16)
        near_part(p, 0, 4)
        both()

        @pl.when(p == 0)
        def _():
            turn(32, 96)
            narrow()

        near_part(p, 4, 8)
        both()
        both()
        both()
        both()
        return carry

    lax.fori_loop(0, 2, product, 0)
    first_out[...] = v[1, 1:9]
    second_out[...] = v[2, 1:9]


def local(charges, basis, transfer, near_field, coupling, ranks, block_source, block_target):
    vmem = pl.BlockSpec(memory_space=pltpu.VMEM)
    hbm = pl.BlockSpec(memory_space=pl.ANY)
    result = jax.ShapeDtypeStruct((8, RHS, LEAF), BF16)
    return pl.pallas_call(
        kernel,
        out_shape=(result, result),
        in_specs=[vmem, vmem, vmem, hbm, hbm, vmem, vmem, vmem],
        out_specs=(vmem, vmem),
        scratch_shapes=[
            pltpu.VMEM((8, 3, LEAF, LEAF), BF16),
            pltpu.VMEM((RMAX, RMAX, BLOCKS), BF16),
            pltpu.VMEM((BLOCKS * RMAX, 128), F32),
            pltpu.VMEM((BLOCKS, RMAX, RMAX), BF16),
            pltpu.VMEM((3, 10, RHS, LEAF), BF16),
            pltpu.VMEM((8, RHS, LEAF), F32),
            pltpu.VMEM((16, 128), F32),
            pltpu.VMEM((8, 128), jnp.int32),
            pltpu.VMEM((3, 64, 128), jnp.int32),
            pltpu.VMEM((2, 2, 8, 128), F32),
            pltpu.VMEM((3, 256, 256), BF16),
            pltpu.VMEM((3, 256, 256), BF16),
            pltpu.VMEM((3, 128, 256), BF16),
            pltpu.VMEM((3, 256, 128), BF16),
            pltpu.VMEM((2, PART * 16, 128), F32),
            pltpu.VMEM((2, PART * BLOCKS, 128), F32),
            pltpu.VMEM((2, PART * BLOCKS, 128), F32),
            pltpu.VMEM((2, 3, BLOCKS, WIDE), BF16),
            pltpu.VMEM((2, 2, 3, 16, 16, WIDE), BF16),
            pltpu.VMEM((2, 2, 2, 3, GROUPS, SLOTS, WIDE), BF16),
            pltpu.VMEM((2, 2, 2, 3, GROUPS, SLOTS, WIDE), BF16),
            pltpu.VMEM((2, 2, 3, 4, 64, WIDE), BF16),
            pltpu.VMEM((2, 2, 3, 3, 64, WIDE), BF16),
            pltpu.VMEM((2, 2, 3, 4, 16, WIDE), BF16),
            pltpu.VMEM((2, 2, 3, 3, 16, WIDE), BF16),
            pltpu.SemaphoreType.DMA((2, 2, COPIES)),
            pltpu.SemaphoreType.DMA((2, 2, COPIES)),
            pltpu.SemaphoreType.DMA((21,)),
            pltpu.SemaphoreType.DMA((21,)),
            pltpu.SemaphoreType.DMA((2,)),
        ],
        compiler_params=pltpu.CompilerParams(
            collective_id=0, has_side_effects=True, vmem_limit_bytes=60 * 1024 * 1024
        ),
    )(charges, basis, transfer, near_field, jnp.transpose(coupling, (1, 2, 0)),
      ranks.reshape(1, 12), block_source.reshape(1, BLOCKS), block_target.reshape(1, BLOCKS))


def solution(mesh):
    in_specs = (
        P("clu", None, None),
        P("clu", None, None),
        P("clu", None, None),
        P("clu", None, None, None),
        P("clu", None, None),
        P("clu"),
        P("clu"),
        P("clu"),
    )
    out_specs = (P("clu", None, None), P("clu", None, None))
    return jax.shard_map(local, mesh=mesh, in_specs=in_specs, out_specs=out_specs, check_vma=False)
```

time: 349 us -> 110 us (0.32)
  waiting for transfers between devices: 151 us -> 0 us
  Pallas kernels: 0 us -> 106 us
  local copies, waits for them, and re-layouts: 99.4 us -> 3.14 us
  starting transfers between devices: 38.4 us -> 0 us
  matrix products: 27.7 us -> 0 us
  other arithmetic: 16 us -> 0 us
  between operations: 14.4 us -> 0.64 us
    all_gather x2 -> x0, waiting for transfers between devices: 128 us -> none  [apply_matrix(): sources = pick_rows(lax.all_gather(coeffs, 'clu', axis=0, tiled=True))]
    pallas_call x0 -> x1, Pallas kernels: none -> 106 us  [local(): pl.pallas_call(kernel, out_shape=(result, result), in_specs=[vmem, vmem,...]
    unnamed x31 -> x2, local copies, waits for them, and re-layouts: 33.8 us -> 3.14 us
    dot_general x18 -> x0, matrix products: 27.7 us -> none  [the longest x4 9 us: apply_matrix(): jnp.einsum('irb,iba->ira', padded[offset:offset + leaves], near_field[:,...]
    all_to_all x3 -> x0, starting transfers between devices: 27.1 us -> none  [the longest x2 15.1 us: apply_matrix(): lax.all_to_all(outbound.astype(jnp.bfloat16), 'clu', split_axis=0, concat...]
    gather x4 -> x0, local copies, waits for them, and re-layouts: 20.1 us -> none  [pick_rows(): rows_now = piece[jnp.clip(block_source, 0, piece.shape[0] - 1)]]
    all_to_all x6 -> x0, local copies, waits for them, and re-layouts: 15.5 us -> none  [the longest x4 14.2 us: apply_matrix(): lax.all_to_all(outbound.astype(jnp.bfloat16), 'clu', split_axis=0, concat...]
    all_to_all x3 -> x0, waiting for transfers between devices: 13.8 us -> none  [the longest x2 13.8 us: apply_matrix(): lax.all_to_all(outbound.astype(jnp.bfloat16), 'clu', split_axis=0, concat...]
  transfers between devices with their start and end apart: 9 -> 0, of which waited for: 6 -> 0; matrix products, arithmetic and copies ran while one was open for 22% -> 0% of each run, Pallas kernels for 0% -> 0%
where the time goes in v2:
time: 110 us
  Pallas kernels  106 us (96%)
  local copies, waits for them, and re-layouts  3.14 us (3%)
    pallas_call x1, Pallas kernels, local(): pl.pallas_call(kernel, out_shape=(result, result), in_specs=[vmem, vmem,...  106 us
    unnamed x2, local copies, waits for them, and re-layouts  3.14 us

profile of v2, /device:TPU:1, one launch (start us, length us, event | category | flops | bytes accessed | tf_op | source)
XLA Modules:
  0.0 110.2 jit_solution(10639590085616583738)
XLA Ops:
  0.6 106.5 %shard_map.95 = (bf16[8,32,256]{2,1,0:T(8,128)(2,1)}, bf16[8,32,256]{2,1,0:T(8,128)(2,1)}) custom-call(bf16[8,32,256]{2,1,0:T(8,128)(2,1)} %charges.1, bf16[8,96,256]{2,1,0:T(8,128)(2,1)} %basis.1, bf16[8,96,96]{2,1,0:T(8,128)(2,1)} %transfer.1, bf16[8,3,256,256]{3,2,1,0:T(8,128)(2,1)} %near_hbm.1, bf16[96,96,128]{2,1,0:T(8,128)(2,1)} %bitcast.4, ...), custom_call_target="tpu_custom_call" | custom-call | tf_op jit(solution)/shard_map/pallas_call | solution.py:451
  107.1 1.6 %copy.12 = bf16[8,32,256]{2,1,0:T(8,128)(2,1)} copy(bf16[8,32,256]{2,1,0:T(8,128)(2,1)} %get-tuple-element.4) | data formatting | bytes 262144
  108.7 1.6 %copy.13 = bf16[8,32,256]{2,1,0:T(8,128)(2,1)} copy(bf16[8,32,256]{2,1,0:T(8,128)(2,1)} %get-tuple-element.5) | data formatting | bytes 262144

commit v3 on v2

v3 whole, which is shorter than its diff:
```python
import jax
import jax.numpy as jnp
from jax import lax
from jax.experimental import pallas as pl
from jax.experimental.pallas import tpu as pltpu
from jax.sharding import PartitionSpec as P

MESH = pl.DeviceIdType.MESH
F32 = jnp.float32
BF16 = jnp.bfloat16
RMAX = 96
RHS = 32
PART = 16
LEAF = 256
STRIDE = {"x": 32, "z": 8, "y": 2}
ROUTES = (("y", "x", "z"), ("z", "y", "x"), ("x", "z", "y"))
STEPS = (2, 1, -1)
WIDE = 512
GROUPS = 8
SLOTS = 32
BLOCKS = 128

G1, G2, EX, R2, R1, HALO = 0, 9, 27, 65, 74, 83
COPIES = 85


def dot(a, b):
    return jnp.dot(a, b, preferred_element_type=F32)


def dot_nt(a, b):
    return lax.dot_general(a, b, (((1,), (1,)), ((), ())), preferred_element_type=F32)


def iota(shape, dim):
    return lax.broadcasted_iota(jnp.int32, shape, dim)


def ones_where(hit):
    return jnp.where(hit, 1.0, 0.0).astype(F32)


def merge(row, extra, u):
    return jnp.where(iota(row.shape, 1) < RMAX, row, pltpu.roll(extra, RMAX - 32 * u, 1))


def fourth(parts):
    rolled = [pltpu.roll(part, 32 + 32 * u, 1) for u, part in enumerate(parts)]
    lanes = iota(parts[0].shape, 1)
    return jnp.where(lanes < 32, rolled[0], jnp.where(lanes < 64, rolled[1], rolled[2]))


def kernel(
    charges_hbm, basis_hbm, transfer_hbm, near_hbm, coupling_hbm, ranks_hbm, source_hbm, target_hbm,
    out,
    basis, transfer, near, turned, wide_coupling, coupling, v, near_sum, ranks, block_source, block_target,
    mask, raw, raw_in, pick, scatter, unpick, place,
    small, big_in, big_out, products, gathered, outbox, inbox, sums_out, sums_in, ends_out, ends_in,
    send_sem, recv_sem, list_send, list_recv, load_sem,
):
    me = lax.axis_index("clu")
    devices = 128
    core = lax.rem(me, 2)
    pos = {a: lax.rem(lax.div(me, s), 4) for a, s in STRIDE.items()}

    def near_by(axis, step, other=0):
        base = me + (lax.rem(pos[axis] + (step + 4), 4) - pos[axis]) * STRIDE[axis]
        return base + (1 - 2 * core) if other else base

    sibling = me + (1 - 2 * core)
    before = lax.rem(me + devices - 1, devices)
    after = lax.rem(me + 1, devices)

    barrier = pltpu.get_barrier_semaphore()
    peers = [sibling, before, after]
    for axis in STRIDE:
        for step in STEPS:
            for other in (0, 1):
                peers.append(near_by(axis, step, other))
    for peer in peers:
        pl.semaphore_signal(barrier, inc=1, device_id=(peer,), device_id_type=MESH)

    loads = [pltpu.make_async_copy(src, dst, load_sem.at[k]) for k, (src, dst) in enumerate((
        (charges_hbm, v.at[0, pl.ds(1, 8)]), (basis_hbm, basis), (transfer_hbm, transfer), (ranks_hbm, ranks),
        (source_hbm, block_source), (target_hbm, block_target), (coupling_hbm, turned), (near_hbm, near)))]
    for load in loads:
        load.start()
    load_coupling, load_near = loads[6:]
    small[...] = jnp.zeros_like(small)
    raw[...] = jnp.zeros_like(raw)

    def copy_of(p, h, k, src, dst, device):
        return pltpu.make_async_remote_copy(
            src_ref=src, dst_ref=dst, send_sem=send_sem.at[p, h, k], recv_sem=recv_sem.at[p, h, k],
            device_id=(device,), device_id_type=MESH)

    def coefficients(p, h):
        rows = pl.ds(PART * h, PART)
        masks = [mask[i : i + 1, :RMAX] for i in range(12)]
        leaves = [dot_nt(v[p, 1 + i, rows], basis[i]) for i in range(8)]
        leaves = [(c * m).astype(BF16) for c, m in zip(leaves, masks)]
        lifted = [dot(c, transfer[i]) for i, c in enumerate(leaves)]
        above = [((lifted[2 * q] + lifted[2 * q + 1]) * masks[8 + q]).astype(BF16) for q in range(4)]
        for i, c in enumerate(leaves + above):
            small[h, pl.ds(i, PART, stride=16), 0:RMAX] = c.astype(F32)
        for u in range(3):
            for g in range(4):
                row = small[h, (4 * g + u) * 16 : (4 * g + u + 1) * 16, :]
                extra = small[h, (4 * g + 3) * 16 : (4 * g + 4) * 16, :]
                gathered[p, h, u, 0, 0, :, g * 128 : (g + 1) * 128] = merge(row, extra, u).astype(BF16)

    def halo_copies(p, h):
        rows = pl.ds(PART * h, PART)
        return [
            copy_of(p, h, HALO, v.at[p, 1, rows], v.at[p, 9, rows], before),
            copy_of(p, h, HALO + 1, v.at[p, 8, rows], v.at[p, 0, rows], after),
        ]

    def first_gather(p, h):
        copies = []
        for u, (first, _, _) in enumerate(ROUTES):
            block = gathered.at[p, h, u, 0]
            copies.append([copy_of(p, h, G1 + 3 * u + s, block.at[0], block.at[-step % 4], near_by(first, step))
                           for s, step in enumerate(STEPS)])
        return copies

    def second_gather(p, h, u, piece):
        second = ROUTES[u][1]
        copies = []
        for s, step in enumerate(STEPS):
            src, dst = gathered.at[p, h, u, 0], gathered.at[p, h, u, -step % 4]
            src, dst = (r.at[pl.ds(1, 3)] if piece else r.at[0] for r in (src, dst))
            copies.append(copy_of(p, h, G2 + (2 * u + piece) * 3 + s, src, dst, near_by(second, step)))
        return copies

    def begin(p, h):
        for copies in first_gather(p, h):
            for copy in copies:
                copy.start()
        for u in range(3):
            for copy in second_gather(p, h, u, 0):
                copy.start()
        for copy in halo_copies(p, h):
            copy.start()

    def near_part(p, lo, hi):
        def body(i, carry):
            s = dot(v[p, i], near[i, 0])
            s = s + dot(v[p, i + 1], near[i, 1])
            near_sum[i] = s + dot(v[p, i + 2], near[i, 2])
            return carry

        lax.fori_loop(lo, hi, body, 0)

    list_copies = []
    for u, (_, _, axis) in enumerate(ROUTES):
        targets = [(near_by(axis, step, o), -step % 4 * 2 + o) for step in STEPS for o in (0, 1)] + [(sibling, 1)]
        for k, (device, group) in enumerate(targets):
            list_copies.append(pltpu.make_async_remote_copy(
                src_ref=raw, dst_ref=raw_in.at[u, pl.ds(8 * group, 8)],
                send_sem=list_send.at[u * 7 + k], recv_sem=list_recv.at[u * 7 + k],
                device_id=(device,), device_id_type=MESH))

    def place_of(ids, route):
        first, second, axis = route
        device = lax.shift_right_logical(ids * 43691, 19)
        where = {a: (lax.shift_right_logical(device, n) + (4 - pos[a])) & 3 for a, n in (("x", 5), ("z", 3), ("y", 1))}
        group = where[axis] * 2 + ((device + core) & 1)
        return group, where[second] * 64 + where[first] * 16 + (ids - 12 * device)

    def make_selectors():
        ahead = ones_where(iota((128, 128), 0) < iota((128, 128), 1)).astype(BF16)
        number = iota((256, 128), 0).astype(F32)
        lines = iota((256, 256), 1).astype(F32)
        within = iota((SLOTS, 128), 0).astype(F32)
        for u, route in enumerate(ROUTES):
            group, _ = place_of(raw[...], route)
            slots = []
            for k in range(2):
                hit = ones_where(iota((8, 128), 0) == group[k : k + 1, :])
                rank = jnp.sum(hit * dot(hit.astype(BF16), ahead), axis=0, keepdims=True)
                slots.append(group[k : k + 1, :].astype(F32) * SLOTS + rank)
            unpick[u] = jnp.transpose(ones_where(number == slots[0]), (1, 0)).astype(BF16)
            place[u] = ones_where(number == slots[1]).astype(BF16)
            raw_in[u, 0:8, :] = raw[...]
            for k in range(2):
                ids = raw_in[u, pl.ds(k, 8, stride=8), :]
                group, row = place_of(ids, route)
                hit = ones_where(group == 0)
                rank = jnp.where(group == 0, dot(hit.astype(BF16), ahead), -1.0)
                row = row.astype(F32) + 1.0
                wanted = []
                for q in range(GROUPS):
                    mine = jnp.where(within == rank[q : q + 1, :], row[q : q + 1, :], 0.0)
                    wanted.append(jnp.sum(mine, axis=1, keepdims=True))
                wanted = jnp.concatenate(wanted, axis=0) - 1.0
                lists = ones_where(lines == wanted)
                if k == 0:
                    pick[u] = lists.astype(BF16)
                else:
                    scatter[u] = jnp.transpose(lists, (1, 0)).astype(BF16)

    def turn(lo, hi):
        same = ones_where(iota((128, 128), 0) == iota((128, 128), 1)).astype(BF16)

        def body(n, carry):
            for k in range(4):
                row = 4 * n + k
                wide_coupling[pl.ds(row, BLOCKS, stride=RMAX), 0:RMAX] = dot_nt(same, turned[row])
            return carry

        lax.fori_loop(lo // 4, hi // 4, body, 0)

    def narrow():
        def body(n, carry):
            for k in range(4):
                j = 4 * n + k
                rows = pl.ds(pl.multiple_of(j * RMAX, RMAX), RMAX)
                coupling[j] = wide_coupling[rows, 0:RMAX].astype(BF16)
            return carry

        lax.fori_loop(0, BLOCKS // 4, body, 0)

    def exchange(p, h, way, u):
        axis = ROUTES[u][2]
        base = EX + 19 * way + 6 * u
        box, to = outbox.at[p, h, way, u], inbox.at[p, h, way, u]
        copies = []
        for s, step in enumerate(STEPS):
            for o in (0, 1):
                copies.append(copy_of(p, h, base + 2 * s + o, box.at[step % 4 * 2 + o], to.at[-step % 4 * 2 + o],
                                      near_by(axis, step, o)))
        for copy in copies:
            copy.start()
        inbox[p, h, way, u, 0] = outbox[p, h, way, u, 0]
        return copies

    def exchange_sibling(p, h, way):
        copy = copy_of(p, h, EX + 19 * way + 18, outbox.at[p, h, way, pl.ds(0, 3), 1],
                       inbox.at[p, h, way, pl.ds(0, 3), 1], sibling)
        copy.start()
        return copy

    def tiles(body):
        lax.fori_loop(0, WIDE // 256, lambda n, carry: body(pl.ds(pl.multiple_of(n * 256, 256), 256), n), 0)

    def stream(p, h):
        started = []
        ring = first_gather(p, h)
        waits = []
        for u in range(3):
            for copy in ring[u]:
                copy.wait_recv()
            copies = second_gather(p, h, u, 1)
            for copy in copies:
                copy.start()
            waits.append(second_gather(p, h, u, 0) + copies)
            started += ring[u] + waits[u]
        yield
        flight = []
        for u in range(3):
            for copy in waits[u]:
                copy.wait_recv()

            def picks(cols, n, u=u):
                rows = gathered[p, h, u, :, :, :, cols].reshape(256, 256)
                outbox[p, h, 0, u, :, :, cols] = dot(pick[u], rows).astype(BF16).reshape(GROUPS, SLOTS, 256)
                return 0

            tiles(picks)
            flight.append(exchange(p, h, 0, u))
        flight.append([exchange_sibling(p, h, 0)])
        yield
        for copies in flight:
            started += copies
            for copy in copies:
                copy.wait_recv()

        def unpicks(cols, n):
            parts = [dot(unpick[u], inbox[p, h, 0, u, :, :, cols].reshape(256, 256)) for u in range(3)]
            for k in range(2):
                g = 2 * n + k
                sides = [part[:, k * 128 : (k + 1) * 128] for part in parts]
                for u in range(3):
                    big_in[h, pl.ds(pl.multiple_of((4 * g + u) * 128, 128), 128), :] = sides[u]
                big_in[h, pl.ds(pl.multiple_of((4 * g + 3) * 128, 128), 128), :] = fourth(sides)
            return 0

        tiles(unpicks)

        def blocks(b, carry):
            for k in range(16):
                j = b * 16 + k
                x = big_in[h, pl.ds(j, PART, stride=BLOCKS), 0:RMAX].astype(BF16)
                big_out[h, pl.ds(j, PART, stride=BLOCKS), 0:RMAX] = dot(x, coupling[j])
            return carry

        lax.fori_loop(0, BLOCKS // 16, blocks, 0)

        def packs(g, carry):
            cols = pl.ds(pl.multiple_of(g * 128, 128), 128)
            extra = big_out[h, pl.ds(pl.multiple_of((4 * g + 3) * 128, 128), 128), :]
            for u in range(3):
                row = big_out[h, pl.ds(pl.multiple_of((4 * g + u) * 128, 128), 128), :]
                products[h, u, :, cols] = merge(row, extra, u).astype(BF16)
            return carry

        lax.fori_loop(0, 4, packs, 0)
        flight = []
        for u in range(3):
            def places(cols, n, u=u):
                sent = dot(place[u], products[h, u, :, cols]).astype(BF16)
                outbox[p, h, 1, u, :, :, cols] = sent.reshape(GROUPS, SLOTS, 256)
                return 0

            tiles(places)
            flight.append(exchange(p, h, 1, u))
        flight.append([exchange_sibling(p, h, 1)])
        yield
        parts = []
        started += flight[3]
        flight[3][0].wait_recv()
        for u, (_, axis, _) in enumerate(ROUTES):
            started += flight[u]
            for copy in flight[u]:
                copy.wait_recv()

            def sums(cols, n, u=u):
                rows = inbox[p, h, 1, u, :, :, cols].reshape(256, 256)
                sums_out[p, h, u, :, :, cols] = dot(scatter[u], rows).astype(BF16).reshape(4, 64, 256)
                return 0

            tiles(sums)
            copies = [copy_of(p, h, R2 + 3 * u + s, sums_out.at[p, h, u, step % 4], sums_in.at[p, h, u, s],
                              near_by(axis, step)) for s, step in enumerate(STEPS)]
            for copy in copies:
                copy.start()
            parts.append(copies)
        yield
        ends = []
        for u, (axis, _, _) in enumerate(ROUTES):
            started += parts[u]
            for copy in parts[u]:
                copy.wait_recv()
            for k in range(4):
                rows = slice(16 * k, 16 * k + 16)
                s = sums_out[p, h, u, 0, rows].astype(F32)
                for n in range(3):
                    s = s + sums_in[p, h, u, n, rows].astype(F32)
                ends_out[p, h, u, k] = s.astype(BF16)
            copies = [copy_of(p, h, R1 + 3 * u + s, ends_out.at[p, h, u, step % 4], ends_in.at[p, h, u, s],
                              near_by(axis, step)) for s, step in enumerate(STEPS)]
            for copy in copies:
                copy.start()
            ends.append(copies)
        yield
        sides = []
        for u in range(3):
            started += ends[u]
            for copy in ends[u]:
                copy.wait_recv()
            s = ends_out[p, h, u, 0].astype(F32)
            for n in range(3):
                s = s + ends_in[p, h, u, n].astype(F32)
            sides.append(s)
        for g in range(4):
            here = [s[:, g * 128 : (g + 1) * 128] for s in sides]
            for u in range(3):
                small[h, (4 * g + u) * 16 : (4 * g + u + 1) * 16, :] = here[u]
            small[h, (4 * g + 3) * 16 : (4 * g + 4) * 16, :] = fourth(here)
        lines = pl.ds(PART * h, PART)
        masks = [mask[i : i + 1, :RMAX] for i in range(12)]
        fields = [(small[h, pl.ds(i, PART, stride=16), 0:RMAX] * masks[i]).astype(BF16) for i in range(12)]
        downs = [dot_nt(fields[8 + i // 2], transfer[i]) for i in range(8)]
        leaves = [((fields[i].astype(F32) + downs[i]) * masks[i]).astype(BF16) for i in range(8)]
        fars = [dot(leaves[i], basis[i]) for i in range(8)]
        fars = [(near_sum[i, lines] + fars[i]).astype(BF16) for i in range(8)]
        for i in range(8):
            v[p + 1, 1 + i, lines] = fars[i]

        @pl.when(p == 0)
        def _():
            small[h] = jnp.zeros_like(small[h])
            coefficients(p + 1, h)
            begin(p + 1, h)

        for copy in started + halo_copies(p, h):
            copy.wait_send()
        yield

    for load in loads[:6]:
        load.wait()
    raw[0:1, :] = block_source[...]
    raw[1:2, :] = block_target[...]
    for i in range(12):
        mask[i : i + 1, :] = ones_where(iota((1, 128), 1) < ranks[0:1, i : i + 1])
    coefficients(0, 0)
    coefficients(0, 1)
    pl.semaphore_wait(barrier, len(peers))
    for copy in list_copies:
        copy.start()
    begin(0, 0)
    begin(0, 1)

    def product(p, carry):
        streams = [stream(p, h) for h in (0, 1)]

        def both():
            for s in streams:
                next(s)

        @pl.when(p == 0)
        def _():
            for copy in list_copies:
                copy.wait()
            make_selectors()

        both()

        @pl.when(p == 0)
        def _():
            load_coupling.wait()
            turn(0, 32)
            load_near.wait()

        for h in (0, 1):
            for copy in halo_copies(p, h):
                copy.wait_recv()
        v[p, 0] = (v[p, 0].astype(F32) * (me > 0).astype(F32)).astype(BF16)
        v[p, 9] = (v[p, 9].astype(F32) * (me < devices - 1).astype(F32)).astype(BF16)
        near_part(p, 0, 4)
        both()

        @pl.when(p == 0)
        def _():
            turn(32, 96)
            narrow()

        near_part(p, 4, 8)
        both()
        both()
        both()
        both()
        return carry

    lax.fori_loop(0, 2, product, 0)
    out[...] = v[1:3, 1:9]


def local(charges, basis, transfer, near_field, coupling, ranks, block_source, block_target):
    vmem = pl.BlockSpec(memory_space=pltpu.VMEM)
    hbm = pl.BlockSpec(memory_space=pl.ANY)
    both = pl.pallas_call(
        kernel,
        out_shape=jax.ShapeDtypeStruct((2, 8, RHS, LEAF), BF16),
        in_specs=[hbm] * 8,
        out_specs=vmem,
        scratch_shapes=[
            pltpu.VMEM((8, RMAX, LEAF), BF16),
            pltpu.VMEM((8, RMAX, RMAX), BF16),
            pltpu.VMEM((8, 3, LEAF, LEAF), BF16),
            pltpu.VMEM((RMAX, RMAX, BLOCKS), BF16),
            pltpu.VMEM((BLOCKS * RMAX, 128), F32),
            pltpu.VMEM((BLOCKS, RMAX, RMAX), BF16),
            pltpu.VMEM((3, 10, RHS, LEAF), BF16),
            pltpu.VMEM((8, RHS, LEAF), F32),
            pltpu.VMEM((1, 12), jnp.int32),
            pltpu.VMEM((1, BLOCKS), jnp.int32),
            pltpu.VMEM((1, BLOCKS), jnp.int32),
            pltpu.VMEM((16, 128), F32),
            pltpu.VMEM((8, 128), jnp.int32),
            pltpu.VMEM((3, 64, 128), jnp.int32),
            pltpu.VMEM((3, 256, 256), BF16),
            pltpu.VMEM((3, 256, 256), BF16),
            pltpu.VMEM((3, 128, 256), BF16),
            pltpu.VMEM((3, 256, 128), BF16),
            pltpu.VMEM((2, PART * 16, 128), F32),
            pltpu.VMEM((2, PART * BLOCKS, 128), F32),
            pltpu.VMEM((2, PART * BLOCKS, 128), F32),
            pltpu.VMEM((2, 3, BLOCKS, WIDE), BF16),
            pltpu.VMEM((2, 2, 3, 4, 4, 16, WIDE), BF16),
            pltpu.VMEM((2, 2, 2, 3, GROUPS, SLOTS, WIDE), BF16),
            pltpu.VMEM((2, 2, 2, 3, GROUPS, SLOTS, WIDE), BF16),
            pltpu.VMEM((2, 2, 3, 4, 64, WIDE), BF16),
            pltpu.VMEM((2, 2, 3, 3, 64, WIDE), BF16),
            pltpu.VMEM((2, 2, 3, 4, 16, WIDE), BF16),
            pltpu.VMEM((2, 2, 3, 3, 16, WIDE), BF16),
            pltpu.SemaphoreType.DMA((2, 2, COPIES)),
            pltpu.SemaphoreType.DMA((2, 2, COPIES)),
            pltpu.SemaphoreType.DMA((21,)),
            pltpu.SemaphoreType.DMA((21,)),
            pltpu.SemaphoreType.DMA((8,)),
        ],
        compiler_params=pltpu.CompilerParams(
            collective_id=0, has_side_effects=True, vmem_limit_bytes=60 * 1024 * 1024
        ),
    )(charges, basis, transfer, near_field, jnp.transpose(coupling, (1, 2, 0)),
      ranks.reshape(1, 12), block_source.reshape(1, BLOCKS), block_target.reshape(1, BLOCKS))
    return both[0], both[1]


def solution(mesh):
    in_specs = (
        P("clu", None, None),
        P("clu", None, None),
        P("clu", None, None),
        P("clu", None, None, None),
        P("clu", None, None),
        P("clu"),
        P("clu"),
        P("clu"),
    )
    out_specs = (P("clu", None, None), P("clu", None, None))
    return jax.shard_map(local, mesh=mesh, in_specs=in_specs, out_specs=out_specs, check_vma=False)
```

time: 110 us -> 98.4 us (0.89)
  Pallas kernels: 106 us -> 96 us
  local copies, waits for them, and re-layouts: 3.14 us -> 1.68 us
    pallas_call x1, Pallas kernels: 106 us -> 96 us  [local(): pl.pallas_call(kernel, out_shape=jax.ShapeDtypeStruct((2, 8, RHS, LEAF),...]
    unnamed x2 -> x0, local copies, waits for them, and re-layouts: 3.14 us -> none
    squeeze x0 -> x1, local copies, waits for them, and re-layouts: none -> 1.68 us  [local(): return (both[0], both[1])]
where the time goes in v3:
time: 98.4 us; the launch traced here: 98.3 us
  Pallas kernels  96 us (98%)
  local copies, waits for them, and re-layouts  1.68 us (2%)
    pallas_call x1, Pallas kernels, local(): pl.pallas_call(kernel, out_shape=jax.ShapeDtypeStruct((2, 8, RHS, LEAF),...  96 us

profile of v3, /device:TPU:1, one launch (start us, length us, event | category | flops | bytes accessed | tf_op | source)
XLA Modules:
  0.0 98.3 jit_solution(5784100896628446013)
XLA Ops:
  0.6 96.0 %shard_map.95 = bf16[2,8,32,256]{3,2,1,0:T(8,128)(2,1)} custom-call(bf16[8,32,256]{2,1,0:T(8,128)(2,1)} %charges_hbm.1, bf16[8,96,256]{2,1,0:T(8,128)(2,1)} %basis_hbm.1, bf16[8,96,96]{2,1,0:T(8,128)(2,1)} %transfer_hbm.1, bf16[8,3,256,256]{3,2,1,0:T(8,128)(2,1)} %near_hbm.1, bf16[96,96,128]{2,1,0:T(8,128)(2,1)} %bitcast.8, s32[1,12]{1,0:T(1,128)} %bitcast.9, ...), custom_call_target="tpu_custom_call" | custom-call | tf_op jit(solution)/shard_map/pallas_call | solution.py:453
  96.6 1.7 %slice_bitcast_fusion = (bf16[8,32,256]{2,1,0:T(8,128)(2,1)}, bf16[8,32,256]{2,1,0:T(8,128)(2,1)}) fusion(bf16[2,8,32,256]{3,2,1,0:T(8,128)(2,1)} %shard_map.95), kind=kLoop, calls=%fused_computation | loop fusion | bytes 524288 | tf_op jit(solution)/shard_map/squeeze | solution.py:499

commit v4 on v3

--- a/solution.py
+++ b/solution.py
@@ -20,8 +20,8 @@
 SLOTS = 32
 BLOCKS = 128
 
-G1, G2, EX, R2, R1, HALO = 0, 9, 27, 65, 74, 83
-COPIES = 85
+G1, G2, EX, R2, R1, HALO = 0, 3, 6, 12, 15, 18
+GROUPS_OF_COPIES = 19
 
 
 def dot(a, b):
@@ -94,6 +94,9 @@
             src_ref=src, dst_ref=dst, send_sem=send_sem.at[p, h, k], recv_sem=recv_sem.at[p, h, k],
             device_id=(device,), device_id_type=MESH)
 
+    def arrivals(p, h, k, where):
+        return copy_of(p, h, k, where, where, sibling)
+
     def coefficients(p, h):
         rows = pl.ds(PART * h, PART)
         masks = [mask[i : i + 1, :RMAX] for i in range(12)]
@@ -113,14 +116,14 @@
         rows = pl.ds(PART * h, PART)
         return [
             copy_of(p, h, HALO, v.at[p, 1, rows], v.at[p, 9, rows], before),
-            copy_of(p, h, HALO + 1, v.at[p, 8, rows], v.at[p, 0, rows], after),
+            copy_of(p, h, HALO, v.at[p, 8, rows], v.at[p, 0, rows], after),
         ]
 
     def first_gather(p, h):
         copies = []
         for u, (first, _, _) in enumerate(ROUTES):
             block = gathered.at[p, h, u, 0]
-            copies.append([copy_of(p, h, G1 + 3 * u + s, block.at[0], block.at[-step % 4], near_by(first, step))
+            copies.append([copy_of(p, h, G1 + u, block.at[0], block.at[-step % 4], near_by(first, step))
                            for s, step in enumerate(STEPS)])
         return copies
 
@@ -130,7 +133,7 @@
         for s, step in enumerate(STEPS):
             src, dst = gathered.at[p, h, u, 0], gathered.at[p, h, u, -step % 4]
             src, dst = (r.at[pl.ds(1, 3)] if piece else r.at[0] for r in (src, dst))
-            copies.append(copy_of(p, h, G2 + (2 * u + piece) * 3 + s, src, dst, near_by(second, step)))
+            copies.append(copy_of(p, h, G2 + u, src, dst, near_by(second, step)))
         return copies
 
     def begin(p, h):
@@ -144,21 +147,18 @@
             copy.start()
 
     def near_part(p, lo, hi):
-        def body(i, carry):
+        for i in range(lo, hi):
             s = dot(v[p, i], near[i, 0])
             s = s + dot(v[p, i + 1], near[i, 1])
             near_sum[i] = s + dot(v[p, i + 2], near[i, 2])
-            return carry
-
-        lax.fori_loop(lo, hi, body, 0)
 
     list_copies = []
     for u, (_, _, axis) in enumerate(ROUTES):
         targets = [(near_by(axis, step, o), -step % 4 * 2 + o) for step in STEPS for o in (0, 1)] + [(sibling, 1)]
-        for k, (device, group) in enumerate(targets):
+        for device, group in targets:
             list_copies.append(pltpu.make_async_remote_copy(
                 src_ref=raw, dst_ref=raw_in.at[u, pl.ds(8 * group, 8)],
-                send_sem=list_send.at[u * 7 + k], recv_sem=list_recv.at[u * 7 + k],
+                send_sem=list_send.at[u], recv_sem=list_recv.at[u],
                 device_id=(device,), device_id_type=MESH))
 
     def place_of(ids, route):
@@ -200,81 +200,62 @@
                 else:
                     scatter[u] = jnp.transpose(lists, (1, 0)).astype(BF16)
 
-    def turn(lo, hi):
-        same = ones_where(iota((128, 128), 0) == iota((128, 128), 1)).astype(BF16)
-
+    def turn():
         def body(n, carry):
-            for k in range(4):
-                row = 4 * n + k
-                wide_coupling[pl.ds(row, BLOCKS, stride=RMAX), 0:RMAX] = dot_nt(same, turned[row])
+            for k in range(32):
+                row = 32 * n + k
+                wide_coupling[pl.ds(row, BLOCKS, stride=RMAX), 0:RMAX] = jnp.transpose(turned[row].astype(F32), (1, 0))
             return carry
 
-        lax.fori_loop(lo // 4, hi // 4, body, 0)
+        lax.fori_loop(0, RMAX // 32, body, 0)
 
     def narrow():
         def body(n, carry):
-            for k in range(4):
-                j = 4 * n + k
+            for k in range(8):
+                j = 8 * n + k
                 rows = pl.ds(pl.multiple_of(j * RMAX, RMAX), RMAX)
                 coupling[j] = wide_coupling[rows, 0:RMAX].astype(BF16)
             return carry
 
-        lax.fori_loop(0, BLOCKS // 4, body, 0)
+        lax.fori_loop(0, BLOCKS // 8, body, 0)
 
     def exchange(p, h, way, u):
         axis = ROUTES[u][2]
-        base = EX + 19 * way + 6 * u
         box, to = outbox.at[p, h, way, u], inbox.at[p, h, way, u]
-        copies = []
+        targets = [(near_by(axis, step, o), step % 4 * 2 + o, -step % 4 * 2 + o) for step in STEPS for o in (0, 1)]
+        for device, src, dst in targets + [(sibling, 1, 1)]:
+            copy_of(p, h, EX + 3 * way + u, box.at[src], to.at[dst], device).start()
+        inbox[p, h, way, u, 0] = outbox[p, h, way, u, 0]
+
+    def exchanged(p, h, way, u):
+        return arrivals(p, h, EX + 3 * way + u, inbox.at[p, h, way, u, pl.ds(1, 7)])
+
+    def tiles(body):
+        for n in range(WIDE // 256):
+            body(slice(256 * n, 256 * n + 256), n)
+
+    def line_copies(p, h, k, out, into, axis):
         for s, step in enumerate(STEPS):
-            for o in (0, 1):
-                copies.append(copy_of(p, h, base + 2 * s + o, box.at[step % 4 * 2 + o], to.at[-step % 4 * 2 + o],
-                                      near_by(axis, step, o)))
-        for copy in copies:
-            copy.start()
-        inbox[p, h, way, u, 0] = outbox[p, h, way, u, 0]
-        return copies
-
-    def exchange_sibling(p, h, way):
-        copy = copy_of(p, h, EX + 19 * way + 18, outbox.at[p, h, way, pl.ds(0, 3), 1],
-                       inbox.at[p, h, way, pl.ds(0, 3), 1], sibling)
-        copy.start()
-        return copy
-
-    def tiles(body):
-        lax.fori_loop(0, WIDE // 256, lambda n, carry: body(pl.ds(pl.multiple_of(n * 256, 256), 256), n), 0)
+            copy_of(p, h, k, out.at[step % 4], into.at[s], near_by(axis, step)).start()
 
     def stream(p, h):
-        started = []
-        ring = first_gather(p, h)
-        waits = []
-        for u in range(3):
-            for copy in ring[u]:
-                copy.wait_recv()
-            copies = second_gather(p, h, u, 1)
-            for copy in copies:
+        for u in range(3):
+            arrivals(p, h, G1 + u, gathered.at[p, h, u, 0, pl.ds(1, 3)]).wait_recv()
+            for copy in second_gather(p, h, u, 1):
                 copy.start()
-            waits.append(second_gather(p, h, u, 0) + copies)
-            started += ring[u] + waits[u]
-        yield
-        flight = []
-        for u in range(3):
-            for copy in waits[u]:
-                copy.wait_recv()
+        yield
+        for u in range(3):
+            arrivals(p, h, G2 + u, gathered.at[p, h, u, pl.ds(1, 3)]).wait_recv()
 
             def picks(cols, n, u=u):
                 rows = gathered[p, h, u, :, :, :, cols].reshape(256, 256)
                 outbox[p, h, 0, u, :, :, cols] = dot(pick[u], rows).astype(BF16).reshape(GROUPS, SLOTS, 256)
-                return 0
 
             tiles(picks)
-            flight.append(exchange(p, h, 0, u))
-        flight.append([exchange_sibling(p, h, 0)])
-        yield
-        for copies in flight:
-            started += copies
-            for copy in copies:
-                copy.wait_recv()
+            exchange(p, h, 0, u)
+        yield
+        for u in range(3):
+            exchanged(p, h, 0, u).wait_recv()
 
         def unpicks(cols, n):
             parts = [dot(unpick[u], inbox[p, h, 0, u, :, :, cols].reshape(256, 256)) for u in range(3)]
@@ -282,83 +263,50 @@
                 g = 2 * n + k
                 sides = [part[:, k * 128 : (k + 1) * 128] for part in parts]
                 for u in range(3):
-                    big_in[h, pl.ds(pl.multiple_of((4 * g + u) * 128, 128), 128), :] = sides[u]
-                big_in[h, pl.ds(pl.multiple_of((4 * g + 3) * 128, 128), 128), :] = fourth(sides)
-            return 0
+                    big_in[h, (4 * g + u) * 128 : (4 * g + u + 1) * 128, :] = sides[u]
+                big_in[h, (4 * g + 3) * 128 : (4 * g + 4) * 128, :] = fourth(sides)
 
         tiles(unpicks)
 
-        def blocks(b, carry):
-            for k in range(16):
-                j = b * 16 + k
-                x = big_in[h, pl.ds(j, PART, stride=BLOCKS), 0:RMAX].astype(BF16)
-                big_out[h, pl.ds(j, PART, stride=BLOCKS), 0:RMAX] = dot(x, coupling[j])
-            return carry
-
-        lax.fori_loop(0, BLOCKS // 16, blocks, 0)
-
-        def packs(g, carry):
-            cols = pl.ds(pl.multiple_of(g * 128, 128), 128)
-            extra = big_out[h, pl.ds(pl.multiple_of((4 * g + 3) * 128, 128), 128), :]
+        for j in range(BLOCKS):
+            x = big_in[h, pl.ds(j, PART, stride=BLOCKS), 0:RMAX].astype(BF16)
+            big_out[h, pl.ds(j, PART, stride=BLOCKS), 0:RMAX] = dot(x, coupling[j])
+        for g in range(4):
+            extra = big_out[h, (4 * g + 3) * 128 : (4 * g + 4) * 128, :]
             for u in range(3):
-                row = big_out[h, pl.ds(pl.multiple_of((4 * g + u) * 128, 128), 128), :]
-                products[h, u, :, cols] = merge(row, extra, u).astype(BF16)
-            return carry
-
-        lax.fori_loop(0, 4, packs, 0)
-        flight = []
+                row = big_out[h, (4 * g + u) * 128 : (4 * g + u + 1) * 128, :]
+                products[h, u, :, g * 128 : (g + 1) * 128] = merge(row, extra, u).astype(BF16)
         for u in range(3):
             def places(cols, n, u=u):
                 sent = dot(place[u], products[h, u, :, cols]).astype(BF16)
                 outbox[p, h, 1, u, :, :, cols] = sent.reshape(GROUPS, SLOTS, 256)
-                return 0
 
             tiles(places)
-            flight.append(exchange(p, h, 1, u))
-        flight.append([exchange_sibling(p, h, 1)])
-        yield
-        parts = []
-        started += flight[3]
-        flight[3][0].wait_recv()
+            exchange(p, h, 1, u)
+        yield
         for u, (_, axis, _) in enumerate(ROUTES):
-            started += flight[u]
-            for copy in flight[u]:
-                copy.wait_recv()
+            exchanged(p, h, 1, u).wait_recv()
 
             def sums(cols, n, u=u):
                 rows = inbox[p, h, 1, u, :, :, cols].reshape(256, 256)
                 sums_out[p, h, u, :, :, cols] = dot(scatter[u], rows).astype(BF16).reshape(4, 64, 256)
-                return 0
 
             tiles(sums)
-            copies = [copy_of(p, h, R2 + 3 * u + s, sums_out.at[p, h, u, step % 4], sums_in.at[p, h, u, s],
-                              near_by(axis, step)) for s, step in enumerate(STEPS)]
-            for copy in copies:
-                copy.start()
-            parts.append(copies)
-        yield
-        ends = []
+            line_copies(p, h, R2 + u, sums_out.at[p, h, u], sums_in.at[p, h, u], axis)
+        yield
         for u, (axis, _, _) in enumerate(ROUTES):
-            started += parts[u]
-            for copy in parts[u]:
-                copy.wait_recv()
+            arrivals(p, h, R2 + u, sums_in.at[p, h, u]).wait_recv()
             for k in range(4):
                 rows = slice(16 * k, 16 * k + 16)
                 s = sums_out[p, h, u, 0, rows].astype(F32)
                 for n in range(3):
                     s = s + sums_in[p, h, u, n, rows].astype(F32)
                 ends_out[p, h, u, k] = s.astype(BF16)
-            copies = [copy_of(p, h, R1 + 3 * u + s, ends_out.at[p, h, u, step % 4], ends_in.at[p, h, u, s],
-                              near_by(axis, step)) for s, step in enumerate(STEPS)]
-            for copy in copies:
-                copy.start()
-            ends.append(copies)
+            line_copies(p, h, R1 + u, ends_out.at[p, h, u], ends_in.at[p, h, u], axis)
         yield
         sides = []
         for u in range(3):
-            started += ends[u]
-            for copy in ends[u]:
-                copy.wait_recv()
+            arrivals(p, h, R1 + u, ends_in.at[p, h, u]).wait_recv()
             s = ends_out[p, h, u, 0].astype(F32)
             for n in range(3):
                 s = s + ends_in[p, h, u, n].astype(F32)
@@ -384,8 +332,14 @@
             coefficients(p + 1, h)
             begin(p + 1, h)
 
-        for copy in started + halo_copies(p, h):
-            copy.wait_send()
+        for u in range(3):
+            arrivals(p, h, G1 + u, gathered.at[p, h, u, 0, pl.ds(1, 3)]).wait_send()
+            arrivals(p, h, G2 + u, gathered.at[p, h, u, pl.ds(1, 3)]).wait_send()
+            exchanged(p, h, 0, u).wait_send()
+            exchanged(p, h, 1, u).wait_send()
+            arrivals(p, h, R2 + u, sums_in.at[p, h, u]).wait_send()
+            arrivals(p, h, R1 + u, ends_in.at[p, h, u]).wait_send()
+        arrivals(p, h, HALO, v.at[p, pl.ds(0, 2), lines]).wait_send()
         yield
 
     for load in loads[:6]:
@@ -409,23 +363,23 @@
             for s in streams:
                 next(s)
 
+        both()
+
         @pl.when(p == 0)
         def _():
-            for copy in list_copies:
+            for u in range(3):
+                tiles_in = raw_in.at[u, pl.ds(8, 56)]
+                copy = pltpu.make_async_remote_copy(
+                    src_ref=tiles_in, dst_ref=tiles_in, send_sem=list_send.at[u], recv_sem=list_recv.at[u],
+                    device_id=(sibling,), device_id_type=MESH)
                 copy.wait()
             make_selectors()
-
-        both()
-
-        @pl.when(p == 0)
-        def _():
             load_coupling.wait()
-            turn(0, 32)
+            turn()
             load_near.wait()
 
         for h in (0, 1):
-            for copy in halo_copies(p, h):
-                copy.wait_recv()
+            arrivals(p, h, HALO, v.at[p, pl.ds(0, 2), pl.ds(PART * h, PART)]).wait_recv()
         v[p, 0] = (v[p, 0].astype(F32) * (me > 0).astype(F32)).astype(BF16)
         v[p, 9] = (v[p, 9].astype(F32) * (me < devices - 1).astype(F32)).astype(BF16)
         near_part(p, 0, 4)
@@ -433,7 +387,6 @@
 
         @pl.when(p == 0)
         def _():
-            turn(32, 96)
             narrow()
 
         near_part(p, 4, 8)
@@ -485,10 +438,10 @@
             pltpu.VMEM((2, 2, 3, 3, 64, WIDE), BF16),
             pltpu.VMEM((2, 2, 3, 4, 16, WIDE), BF16),
             pltpu.VMEM((2, 2, 3, 3, 16, WIDE), BF16),
-            pltpu.SemaphoreType.DMA((2, 2, COPIES)),
-            pltpu.SemaphoreType.DMA((2, 2, COPIES)),
-            pltpu.SemaphoreType.DMA((21,)),
-            pltpu.SemaphoreType.DMA((21,)),
+            pltpu.SemaphoreType.DMA((2, 2, GROUPS_OF_COPIES)),
+            pltpu.SemaphoreType.DMA((2, 2, GROUPS_OF_COPIES)),
+            pltpu.SemaphoreType.DMA((3,)),
+            pltpu.SemaphoreType.DMA((3,)),
             pltpu.SemaphoreType.DMA((8,)),
         ],
         compiler_params=pltpu.CompilerParams(

time: 98.4 us -> 83.4 us (0.85)
  Pallas kernels: 96 us -> 80.9 us
    pallas_call x1, Pallas kernels: 96 us -> 80.9 us  [local(): pl.pallas_call(kernel, out_shape=jax.ShapeDtypeStruct((2, 8, RHS, LEAF),...]
where the time goes in v4:
time: 83.4 us; the launch traced here: 83.2 us
  Pallas kernels  80.9 us (97%)
  local copies, waits for them, and re-layouts  1.68 us (2%)
    pallas_call x1, Pallas kernels, local(): pl.pallas_call(kernel, out_shape=jax.ShapeDtypeStruct((2, 8, RHS, LEAF),...  80.9 us
    squeeze x1, local copies, waits for them, and re-layouts, local(): return (both[0], both[1])  1.68 us

profile of v4, /device:TPU:1, one launch (start us, length us, event | category | flops | bytes accessed | tf_op | source)
XLA Modules:
  0.0 83.2 jit_solution(14239377145798066091)
XLA Ops:
  0.6 80.9 %shard_map.95 = bf16[2,8,32,256]{3,2,1,0:T(8,128)(2,1)} custom-call(bf16[8,32,256]{2,1,0:T(8,128)(2,1)} %charges_hbm.1, bf16[8,96,256]{2,1,0:T(8,128)(2,1)} %basis_hbm.1, bf16[8,96,96]{2,1,0:T(8,128)(2,1)} %transfer_hbm.1, bf16[8,3,256,256]{3,2,1,0:T(8,128)(2,1)} %near_hbm.1, bf16[96,96,128]{2,1,0:T(8,128)(2,1)} %bitcast.8, s32[1,12]{1,0:T(1,128)} %bitcast.9, ...), custom_call_target="tpu_custom_call" | custom-call | tf_op jit(solution)/shard_map/pallas_call | solution.py:406
  81.5 1.7 %slice_bitcast_fusion = (bf16[8,32,256]{2,1,0:T(8,128)(2,1)}, bf16[8,32,256]{2,1,0:T(8,128)(2,1)}) fusion(bf16[2,8,32,256]{3,2,1,0:T(8,128)(2,1)} %shard_map.95), kind=kLoop, calls=%fused_computation | loop fusion | bytes 524288 | tf_op jit(solution)/shard_map/squeeze | solution.py:452

commit v5 on v4

--- a/solution.py
+++ b/solution.py
@@ -21,7 +21,9 @@
 BLOCKS = 128
 
 G1, G2, EX, R2, R1, HALO = 0, 3, 6, 12, 15, 18
-GROUPS_OF_COPIES = 19
+ARRIVALS = 19
+KINDS = {G1: 0, G2: 1, EX: 2, EX + 3: 3, R2: 4, R1: 5, HALO: 6}
+ROWS = 48
 
 
 def dot(a, b):
@@ -55,7 +57,7 @@
     out,
     basis, transfer, near, turned, wide_coupling, coupling, v, near_sum, ranks, block_source, block_target,
     mask, raw, raw_in, pick, scatter, unpick, place,
-    small, big_in, big_out, products, gathered, outbox, inbox, sums_out, sums_in, ends_out, ends_in,
+    small, big_in, big_out, products, compact, expand, gathered, packed, outbox, inbox, sums_out, sums_in, ends_out, ends_in,
     send_sem, recv_sem, list_send, list_recv, load_sem,
 ):
     me = lax.axis_index("clu")
@@ -89,13 +91,16 @@
     small[...] = jnp.zeros_like(small)
     raw[...] = jnp.zeros_like(raw)
 
-    def copy_of(p, h, k, src, dst, device):
+    def copy_of(h, k, u, src, dst, device):
         return pltpu.make_async_remote_copy(
-            src_ref=src, dst_ref=dst, send_sem=send_sem.at[p, h, k], recv_sem=recv_sem.at[p, h, k],
+            src_ref=src, dst_ref=dst, send_sem=send_sem.at[h, KINDS[k]], recv_sem=recv_sem.at[h, k + u],
             device_id=(device,), device_id_type=MESH)
 
-    def arrivals(p, h, k, where):
-        return copy_of(p, h, k, where, where, sibling)
+    def arrived(h, k, u, where):
+        copy_of(h, k, u, where, where, sibling).wait_recv()
+
+    def sent(h, k, where):
+        copy_of(h, k, 0, where, where, sibling).wait_send()
 
     def coefficients(p, h):
         rows = pl.ds(PART * h, PART)
@@ -110,43 +115,23 @@
             for g in range(4):
                 row = small[h, (4 * g + u) * 16 : (4 * g + u + 1) * 16, :]
                 extra = small[h, (4 * g + 3) * 16 : (4 * g + 4) * 16, :]
-                gathered[p, h, u, 0, 0, :, g * 128 : (g + 1) * 128] = merge(row, extra, u).astype(BF16)
-
-    def halo_copies(p, h):
+                gathered[p, h, u, 0, :, g * 128 : (g + 1) * 128] = merge(row, extra, u).astype(BF16)
+
+    def begin(p, h):
+        for u, (axis, _, _) in enumerate(ROUTES):
+            block = gathered.at[p, h, u]
+            for step in STEPS:
+                copy_of(h, G1, u, block.at[0], block.at[-step % 4], near_by(axis, step)).start()
         rows = pl.ds(PART * h, PART)
-        return [
-            copy_of(p, h, HALO, v.at[p, 1, rows], v.at[p, 9, rows], before),
-            copy_of(p, h, HALO, v.at[p, 8, rows], v.at[p, 0, rows], after),
-        ]
-
-    def first_gather(p, h):
-        copies = []
-        for u, (first, _, _) in enumerate(ROUTES):
-            block = gathered.at[p, h, u, 0]
-            copies.append([copy_of(p, h, G1 + u, block.at[0], block.at[-step % 4], near_by(first, step))
-                           for s, step in enumerate(STEPS)])
-        return copies
-
-    def second_gather(p, h, u, piece):
-        second = ROUTES[u][1]
-        copies = []
-        for s, step in enumerate(STEPS):
-            src, dst = gathered.at[p, h, u, 0], gathered.at[p, h, u, -step % 4]
-            src, dst = (r.at[pl.ds(1, 3)] if piece else r.at[0] for r in (src, dst))
-            copies.append(copy_of(p, h, G2 + u, src, dst, near_by(second, step)))
-        return copies
-
-    def begin(p, h):
-        for copies in first_gather(p, h):
-            for copy in copies:
-                copy.start()
-        for u in range(3):
-            for copy in second_gather(p, h, u, 0):
-                copy.start()
-        for copy in halo_copies(p, h):
-            copy.start()
+        copy_of(h, HALO, 0, v.at[p, 1, rows], v.at[p, 9, rows], before).start()
+        copy_of(h, HALO, 0, v.at[p, 8, rows], v.at[p, 0, rows], after).start()
 
     def near_part(p, lo, hi):
+        if lo == 0:
+            for h in (0, 1):
+                arrived(h, HALO, 0, v.at[p, pl.ds(0, 2), pl.ds(PART * h, PART)])
+            v[p, 0] = (v[p, 0].astype(F32) * (me > 0).astype(F32)).astype(BF16)
+            v[p, 9] = (v[p, 9].astype(F32) * (me < devices - 1).astype(F32)).astype(BF16)
         for i in range(lo, hi):
             s = dot(v[p, i], near[i, 0])
             s = s + dot(v[p, i + 1], near[i, 1])
@@ -166,13 +151,29 @@
         device = lax.shift_right_logical(ids * 43691, 19)
         where = {a: (lax.shift_right_logical(device, n) + (4 - pos[a])) & 3 for a, n in (("x", 5), ("z", 3), ("y", 1))}
         group = where[axis] * 2 + ((device + core) & 1)
-        return group, where[second] * 64 + where[first] * 16 + (ids - 12 * device)
-
-    def make_selectors():
-        ahead = ones_where(iota((128, 128), 0) < iota((128, 128), 1)).astype(BF16)
+        return group, where[second] * ROWS + where[first] * 12 + (ids - 12 * device)
+
+    ahead = ones_where(iota((128, 128), 0) < iota((128, 128), 1)).astype(BF16)
+
+    def rows_wanted(u, k):
+        within = iota((SLOTS, 128), 0).astype(F32)
+        group, row = place_of(raw_in[u, pl.ds(k, 8, stride=8), :], ROUTES[u])
+        rank = jnp.where(group == 0, dot(ones_where(group == 0).astype(BF16), ahead), -1.0)
+        row = row.astype(F32) + 1.0
+        wanted = []
+        for q in range(GROUPS):
+            mine = jnp.where(within == rank[q : q + 1, :], row[q : q + 1, :], 0.0)
+            wanted.append(jnp.sum(mine, axis=1, keepdims=True))
+        wanted = jnp.concatenate(wanted, axis=0) - 1.0
+        return ones_where(iota((256, 4 * ROWS), 1).astype(F32) == wanted)
+
+    def make_picks():
+        for u in range(3):
+            raw_in[u, 0:8, :] = raw[...]
+            pick[u] = rows_wanted(u, 0).astype(BF16)
+
+    def make_others():
         number = iota((256, 128), 0).astype(F32)
-        lines = iota((256, 256), 1).astype(F32)
-        within = iota((SLOTS, 128), 0).astype(F32)
         for u, route in enumerate(ROUTES):
             group, _ = place_of(raw[...], route)
             slots = []
@@ -182,23 +183,7 @@
                 slots.append(group[k : k + 1, :].astype(F32) * SLOTS + rank)
             unpick[u] = jnp.transpose(ones_where(number == slots[0]), (1, 0)).astype(BF16)
             place[u] = ones_where(number == slots[1]).astype(BF16)
-            raw_in[u, 0:8, :] = raw[...]
-            for k in range(2):
-                ids = raw_in[u, pl.ds(k, 8, stride=8), :]
-                group, row = place_of(ids, route)
-                hit = ones_where(group == 0)
-                rank = jnp.where(group == 0, dot(hit.astype(BF16), ahead), -1.0)
-                row = row.astype(F32) + 1.0
-                wanted = []
-                for q in range(GROUPS):
-                    mine = jnp.where(within == rank[q : q + 1, :], row[q : q + 1, :], 0.0)
-                    wanted.append(jnp.sum(mine, axis=1, keepdims=True))
-                wanted = jnp.concatenate(wanted, axis=0) - 1.0
-                lists = ones_where(lines == wanted)
-                if k == 0:
-                    pick[u] = lists.astype(BF16)
-                else:
-                    scatter[u] = jnp.transpose(lists, (1, 0)).astype(BF16)
+            scatter[u] = jnp.transpose(rows_wanted(u, 1), (1, 0)).astype(BF16)
 
     def turn():
         def body(n, carry):
@@ -224,38 +209,40 @@
         box, to = outbox.at[p, h, way, u], inbox.at[p, h, way, u]
         targets = [(near_by(axis, step, o), step % 4 * 2 + o, -step % 4 * 2 + o) for step in STEPS for o in (0, 1)]
         for device, src, dst in targets + [(sibling, 1, 1)]:
-            copy_of(p, h, EX + 3 * way + u, box.at[src], to.at[dst], device).start()
+            copy_of(h, EX + 3 * way, u, box.at[src], to.at[dst], device).start()
         inbox[p, h, way, u, 0] = outbox[p, h, way, u, 0]
 
     def exchanged(p, h, way, u):
-        return arrivals(p, h, EX + 3 * way + u, inbox.at[p, h, way, u, pl.ds(1, 7)])
+        arrived(h, EX + 3 * way, u, inbox.at[p, h, way, u, pl.ds(1, 7)])
 
     def tiles(body):
         for n in range(WIDE // 256):
             body(slice(256 * n, 256 * n + 256), n)
 
-    def line_copies(p, h, k, out, into, axis):
+    def line_copies(h, k, u, out, into, axis):
         for s, step in enumerate(STEPS):
-            copy_of(p, h, k, out.at[step % 4], into.at[s], near_by(axis, step)).start()
+            copy_of(h, k, u, out.at[step % 4], into.at[s], near_by(axis, step)).start()
 
     def stream(p, h):
-        for u in range(3):
-            arrivals(p, h, G1 + u, gathered.at[p, h, u, 0, pl.ds(1, 3)]).wait_recv()
-            for copy in second_gather(p, h, u, 1):
-                copy.start()
-        yield
-        for u in range(3):
-            arrivals(p, h, G2 + u, gathered.at[p, h, u, pl.ds(1, 3)]).wait_recv()
+        for u, (_, axis, _) in enumerate(ROUTES):
+            arrived(h, G1, u, gathered.at[p, h, u, pl.ds(1, 3)])
+            plane = packed.at[p, h, u]
+            packed[p, h, u, 0] = dot(compact[...], gathered[p, h, u].reshape(64, WIDE)).astype(BF16)
+            for step in STEPS:
+                copy_of(h, G2, u, plane.at[0], plane.at[-step % 4], near_by(axis, step)).start()
+        yield
+        for u in range(3):
+            arrived(h, G2, u, packed.at[p, h, u, pl.ds(1, 3)])
 
             def picks(cols, n, u=u):
-                rows = gathered[p, h, u, :, :, :, cols].reshape(256, 256)
+                rows = packed[p, h, u, :, :, cols].reshape(4 * ROWS, 256)
                 outbox[p, h, 0, u, :, :, cols] = dot(pick[u], rows).astype(BF16).reshape(GROUPS, SLOTS, 256)
 
             tiles(picks)
             exchange(p, h, 0, u)
         yield
         for u in range(3):
-            exchanged(p, h, 0, u).wait_recv()
+            exchanged(p, h, 0, u)
 
         def unpicks(cols, n):
             parts = [dot(unpick[u], inbox[p, h, 0, u, :, :, cols].reshape(256, 256)) for u in range(3)]
@@ -278,35 +265,33 @@
                 products[h, u, :, g * 128 : (g + 1) * 128] = merge(row, extra, u).astype(BF16)
         for u in range(3):
             def places(cols, n, u=u):
-                sent = dot(place[u], products[h, u, :, cols]).astype(BF16)
-                outbox[p, h, 1, u, :, :, cols] = sent.reshape(GROUPS, SLOTS, 256)
+                terms = dot(place[u], products[h, u, :, cols]).astype(BF16)
+                outbox[p, h, 1, u, :, :, cols] = terms.reshape(GROUPS, SLOTS, 256)
 
             tiles(places)
             exchange(p, h, 1, u)
         yield
         for u, (_, axis, _) in enumerate(ROUTES):
-            exchanged(p, h, 1, u).wait_recv()
+            exchanged(p, h, 1, u)
 
             def sums(cols, n, u=u):
                 rows = inbox[p, h, 1, u, :, :, cols].reshape(256, 256)
-                sums_out[p, h, u, :, :, cols] = dot(scatter[u], rows).astype(BF16).reshape(4, 64, 256)
+                sums_out[p, h, u, :, :, cols] = dot(scatter[u], rows).astype(BF16).reshape(4, ROWS, 256)
 
             tiles(sums)
-            line_copies(p, h, R2 + u, sums_out.at[p, h, u], sums_in.at[p, h, u], axis)
+            line_copies(h, R2, u, sums_out.at[p, h, u], sums_in.at[p, h, u], axis)
         yield
         for u, (axis, _, _) in enumerate(ROUTES):
-            arrivals(p, h, R2 + u, sums_in.at[p, h, u]).wait_recv()
-            for k in range(4):
-                rows = slice(16 * k, 16 * k + 16)
-                s = sums_out[p, h, u, 0, rows].astype(F32)
-                for n in range(3):
-                    s = s + sums_in[p, h, u, n, rows].astype(F32)
-                ends_out[p, h, u, k] = s.astype(BF16)
-            line_copies(p, h, R1 + u, ends_out.at[p, h, u], ends_in.at[p, h, u], axis)
+            arrived(h, R2, u, sums_in.at[p, h, u])
+            s = sums_out[p, h, u, 0].astype(F32)
+            for n in range(3):
+                s = s + sums_in[p, h, u, n].astype(F32)
+            ends_out[p, h, u] = dot(expand[...], s.astype(BF16)).astype(BF16).reshape(4, 16, WIDE)
+            line_copies(h, R1, u, ends_out.at[p, h, u], ends_in.at[p, h, u], axis)
         yield
         sides = []
         for u in range(3):
-            arrivals(p, h, R1 + u, ends_in.at[p, h, u]).wait_recv()
+            arrived(h, R1, u, ends_in.at[p, h, u])
             s = ends_out[p, h, u, 0].astype(F32)
             for n in range(3):
                 s = s + ends_in[p, h, u, n].astype(F32)
@@ -326,20 +311,17 @@
         for i in range(8):
             v[p + 1, 1 + i, lines] = fars[i]
 
-        @pl.when(p == 0)
-        def _():
+        sent(h, G1, gathered.at[p, h, :, pl.ds(1, 3)])
+        sent(h, G2, packed.at[p, h, :, pl.ds(1, 3)])
+        sent(h, EX, inbox.at[p, h, 0, :, pl.ds(1, 7)])
+        sent(h, EX + 3, inbox.at[p, h, 1, :, pl.ds(1, 7)])
+        sent(h, R2, sums_in.at[p, h])
+        sent(h, R1, ends_in.at[p, h])
+        sent(h, HALO, v.at[p, pl.ds(0, 2), lines])
+        if p == 0:
             small[h] = jnp.zeros_like(small[h])
-            coefficients(p + 1, h)
-            begin(p + 1, h)
-
-        for u in range(3):
-            arrivals(p, h, G1 + u, gathered.at[p, h, u, 0, pl.ds(1, 3)]).wait_send()
-            arrivals(p, h, G2 + u, gathered.at[p, h, u, pl.ds(1, 3)]).wait_send()
-            exchanged(p, h, 0, u).wait_send()
-            exchanged(p, h, 1, u).wait_send()
-            arrivals(p, h, R2 + u, sums_in.at[p, h, u]).wait_send()
-            arrivals(p, h, R1 + u, ends_in.at[p, h, u]).wait_send()
-        arrivals(p, h, HALO, v.at[p, pl.ds(0, 2), lines]).wait_send()
+            coefficients(1, h)
+            begin(1, h)
         yield
 
     for load in loads[:6]:
@@ -350,13 +332,19 @@
         mask[i : i + 1, :] = ones_where(iota((1, 128), 1) < ranks[0:1, i : i + 1])
     coefficients(0, 0)
     coefficients(0, 1)
+    column, line = iota((ROWS, 64), 1), iota((ROWS, 64), 0)
+    same = lax.shift_right_logical(column, 4) * 12 + (column & 15) == line
+    compact[...] = ones_where(same & ((column & 15) < 12)).astype(BF16)
+    column, line = iota((64, ROWS), 0), iota((64, ROWS), 1)
+    same = lax.shift_right_logical(column, 4) * 12 + (column & 15) == line
+    expand[...] = ones_where(same & ((column & 15) < 12)).astype(BF16)
     pl.semaphore_wait(barrier, len(peers))
     for copy in list_copies:
         copy.start()
     begin(0, 0)
     begin(0, 1)
 
-    def product(p, carry):
+    for p in range(2):
         streams = [stream(p, h) for h in (0, 1)]
 
         def both():
@@ -364,39 +352,28 @@
                 next(s)
 
         both()
-
-        @pl.when(p == 0)
-        def _():
+        if p == 0:
             for u in range(3):
                 tiles_in = raw_in.at[u, pl.ds(8, 56)]
-                copy = pltpu.make_async_remote_copy(
+                pltpu.make_async_remote_copy(
                     src_ref=tiles_in, dst_ref=tiles_in, send_sem=list_send.at[u], recv_sem=list_recv.at[u],
-                    device_id=(sibling,), device_id_type=MESH)
-                copy.wait()
-            make_selectors()
+                    device_id=(sibling,), device_id_type=MESH).wait()
+            make_picks()
+        else:
+            near_part(p, 0, 4)
+        both()
+        if p == 0:
+            make_others()
             load_coupling.wait()
             turn()
+            narrow()
             load_near.wait()
-
-        for h in (0, 1):
-            arrivals(p, h, HALO, v.at[p, pl.ds(0, 2), pl.ds(PART * h, PART)]).wait_recv()
-        v[p, 0] = (v[p, 0].astype(F32) * (me > 0).astype(F32)).astype(BF16)
-        v[p, 9] = (v[p, 9].astype(F32) * (me < devices - 1).astype(F32)).astype(BF16)
-        near_part(p, 0, 4)
-        both()
-
-        @pl.when(p == 0)
-        def _():
-            narrow()
-
+            near_part(p, 0, 4)
         near_part(p, 4, 8)
         both()
         both()
         both()
         both()
-        return carry
-
-    lax.fori_loop(0, 2, product, 0)
     out[...] = v[1:3, 1:9]
 
 
@@ -423,23 +400,26 @@
             pltpu.VMEM((16, 128), F32),
             pltpu.VMEM((8, 128), jnp.int32),
             pltpu.VMEM((3, 64, 128), jnp.int32),
-            pltpu.VMEM((3, 256, 256), BF16),
-            pltpu.VMEM((3, 256, 256), BF16),
+            pltpu.VMEM((3, 256, 4 * ROWS), BF16),
+            pltpu.VMEM((3, 4 * ROWS, 256), BF16),
             pltpu.VMEM((3, 128, 256), BF16),
             pltpu.VMEM((3, 256, 128), BF16),
             pltpu.VMEM((2, PART * 16, 128), F32),
             pltpu.VMEM((2, PART * BLOCKS, 128), F32),
             pltpu.VMEM((2, PART * BLOCKS, 128), F32),
             pltpu.VMEM((2, 3, BLOCKS, WIDE), BF16),
-            pltpu.VMEM((2, 2, 3, 4, 4, 16, WIDE), BF16),
+            pltpu.VMEM((ROWS, 64), BF16),
+            pltpu.VMEM((64, ROWS), BF16),
+            pltpu.VMEM((2, 2, 3, 4, 16, WIDE), BF16),
+            pltpu.VMEM((2, 2, 3, 4, ROWS, WIDE), BF16),
             pltpu.VMEM((2, 2, 2, 3, GROUPS, SLOTS, WIDE), BF16),
             pltpu.VMEM((2, 2, 2, 3, GROUPS, SLOTS, WIDE), BF16),
-            pltpu.VMEM((2, 2, 3, 4, 64, WIDE), BF16),
-            pltpu.VMEM((2, 2, 3, 3, 64, WIDE), BF16),
+            pltpu.VMEM((2, 2, 3, 4, ROWS, WIDE), BF16),
+            pltpu.VMEM((2, 2, 3, 3, ROWS, WIDE), BF16),
             pltpu.VMEM((2, 2, 3, 4, 16, WIDE), BF16),
             pltpu.VMEM((2, 2, 3, 3, 16, WIDE), BF16),
-            pltpu.SemaphoreType.DMA((2, 2, GROUPS_OF_COPIES)),
-            pltpu.SemaphoreType.DMA((2, 2, GROUPS_OF_COPIES)),
+            pltpu.SemaphoreType.DMA((2, len(KINDS))),
+            pltpu.SemaphoreType.DMA((2, ARRIVALS)),
             pltpu.SemaphoreType.DMA((3,)),
             pltpu.SemaphoreType.DMA((3,)),
             pltpu.SemaphoreType.DMA((8,)),

time: 83.4 us -> 81.5 us (0.977)
  Pallas kernels: 80.9 us -> 79 us
    pallas_call x1, Pallas kernels: 80.9 us -> 79 us  [local(): pl.pallas_call(kernel, out_shape=jax.ShapeDtypeStruct((2, 8, RHS, LEAF),...]
where the time goes in v5:
time: 81.5 us; the launch traced here: 81.3 us
  Pallas kernels  79 us (97%)
  local copies, waits for them, and re-layouts  1.68 us (2%)
    pallas_call x1, Pallas kernels, local(): pl.pallas_call(kernel, out_shape=jax.ShapeDtypeStruct((2, 8, RHS, LEAF),...  79 us
    squeeze x1, local copies, waits for them, and re-layouts, local(): return (both[0], both[1])  1.68 us

profile of v5, /device:TPU:1, one launch (start us, length us, event | category | flops | bytes accessed | tf_op | source)
XLA Modules:
  0.0 81.3 jit_solution(6717418703414984050)
XLA Ops:
  0.6 79.0 %shard_map.95 = bf16[2,8,32,256]{3,2,1,0:T(8,128)(2,1)} custom-call(bf16[8,32,256]{2,1,0:T(8,128)(2,1)} %charges_hbm.1, bf16[8,96,256]{2,1,0:T(8,128)(2,1)} %basis_hbm.1, bf16[8,96,96]{2,1,0:T(8,128)(2,1)} %transfer_hbm.1, bf16[8,3,256,256]{3,2,1,0:T(8,128)(2,1)} %near_hbm.1, bf16[96,96,128]{2,1,0:T(8,128)(2,1)} %bitcast.8, s32[1,12]{1,0:T(1,128)} %bitcast.9, ...), custom_call_target="tpu_custom_call" | custom-call | tf_op jit(solution)/shard_map/pallas_call | solution.py:383
  79.6 1.7 %slice_bitcast_fusion = (bf16[8,32,256]{2,1,0:T(8,128)(2,1)}, bf16[8,32,256]{2,1,0:T(8,128)(2,1)}) fusion(bf16[2,8,32,256]{3,2,1,0:T(8,128)(2,1)} %shard_map.95), kind=kLoop, calls=%fused_computation | loop fusion | bytes 524288 | tf_op jit(solution)/shard_map/squeeze | solution.py:432

commit v6 on v5

--- a/solution.py
+++ b/solution.py
@@ -10,20 +10,23 @@
 BF16 = jnp.bfloat16
 RMAX = 96
 RHS = 32
-PART = 16
+STREAMS = 2
+PART = RHS // STREAMS
+QUADS = PART // 4
 LEAF = 256
 STRIDE = {"x": 32, "z": 8, "y": 2}
 ROUTES = (("y", "x", "z"), ("z", "y", "x"), ("x", "z", "y"))
 STEPS = (2, 1, -1)
-WIDE = 512
+WIDE = 128 * QUADS
 GROUPS = 8
 SLOTS = 32
 BLOCKS = 128
 
-G1, G2, EX, R2, R1, HALO = 0, 3, 6, 12, 15, 18
-ARRIVALS = 19
+G1, G2, EX, R2, R1, HALO = 0, 1, 4, 10, 13, 14
+ARRIVALS = 15
 KINDS = {G1: 0, G2: 1, EX: 2, EX + 3: 3, R2: 4, R1: 5, HALO: 6}
 ROWS = 48
+PITCH_BLOCK, PITCH_CLUSTER, PITCH_TURN = 136, 24, 104
 
 
 def dot(a, b):
@@ -55,7 +58,7 @@
 def kernel(
     charges_hbm, basis_hbm, transfer_hbm, near_hbm, coupling_hbm, ranks_hbm, source_hbm, target_hbm,
     out,
-    basis, transfer, near, turned, wide_coupling, coupling, v, near_sum, ranks, block_source, block_target,
+    basis, transfer, near, turned, wide_coupling, coupling, v, lines_of, near_sum, ranks, block_source, block_target,
     mask, raw, raw_in, pick, scatter, unpick, place,
     small, big_in, big_out, products, compact, expand, gathered, packed, outbox, inbox, sums_out, sums_in, ends_out, ends_in,
     send_sem, recv_sem, list_send, list_recv, load_sem,
@@ -103,33 +106,37 @@
         copy_of(h, k, 0, where, where, sibling).wait_send()
 
     def coefficients(p, h):
-        rows = pl.ds(PART * h, PART)
         masks = [mask[i : i + 1, :RMAX] for i in range(12)]
-        leaves = [dot_nt(v[p, 1 + i, rows], basis[i]) for i in range(8)]
+        leaves = [dot_nt(lines_of[h, i].astype(BF16), basis[i]) for i in range(8)]
         leaves = [(c * m).astype(BF16) for c, m in zip(leaves, masks)]
         lifted = [dot(c, transfer[i]) for i, c in enumerate(leaves)]
         above = [((lifted[2 * q] + lifted[2 * q + 1]) * masks[8 + q]).astype(BF16) for q in range(4)]
         for i, c in enumerate(leaves + above):
-            small[h, pl.ds(i, PART, stride=16), 0:RMAX] = c.astype(F32)
-        for u in range(3):
-            for g in range(4):
-                row = small[h, (4 * g + u) * 16 : (4 * g + u + 1) * 16, :]
-                extra = small[h, (4 * g + 3) * 16 : (4 * g + 4) * 16, :]
+            small[h, pl.ds(i, PART, stride=PITCH_CLUSTER), 0:RMAX] = c.astype(F32)
+        for u in range(3):
+            for g in range(QUADS):
+                row = small[h, pl.ds((4 * g + u) * PITCH_CLUSTER, 16), :]
+                extra = small[h, pl.ds((4 * g + 3) * PITCH_CLUSTER, 16), :]
                 gathered[p, h, u, 0, :, g * 128 : (g + 1) * 128] = merge(row, extra, u).astype(BF16)
+
+    def halo_rows(h):
+        return pl.ds(16 * (PART * h // 16), 16)
 
     def begin(p, h):
         for u, (axis, _, _) in enumerate(ROUTES):
             block = gathered.at[p, h, u]
             for step in STEPS:
-                copy_of(h, G1, u, block.at[0], block.at[-step % 4], near_by(axis, step)).start()
-        rows = pl.ds(PART * h, PART)
-        copy_of(h, HALO, 0, v.at[p, 1, rows], v.at[p, 9, rows], before).start()
-        copy_of(h, HALO, 0, v.at[p, 8, rows], v.at[p, 0, rows], after).start()
+                copy_of(h, G1, 0, block.at[0], block.at[-step % 4], near_by(axis, step)).start()
+        if PART * (h + 1) % 16 == 0:
+            rows = halo_rows(h)
+            copy_of(h, HALO, 0, v.at[p, 1, rows], v.at[p, 9, rows], before).start()
+            copy_of(h, HALO, 0, v.at[p, 8, rows], v.at[p, 0, rows], after).start()
 
     def near_part(p, lo, hi):
         if lo == 0:
-            for h in (0, 1):
-                arrived(h, HALO, 0, v.at[p, pl.ds(0, 2), pl.ds(PART * h, PART)])
+            for h in range(STREAMS):
+                if PART * (h + 1) % 16 == 0:
+                    arrived(h, HALO, 0, v.at[p, pl.ds(0, 2), halo_rows(h)])
             v[p, 0] = (v[p, 0].astype(F32) * (me > 0).astype(F32)).astype(BF16)
             v[p, 9] = (v[p, 9].astype(F32) * (me < devices - 1).astype(F32)).astype(BF16)
         for i in range(lo, hi):
@@ -189,7 +196,7 @@
         def body(n, carry):
             for k in range(32):
                 row = 32 * n + k
-                wide_coupling[pl.ds(row, BLOCKS, stride=RMAX), 0:RMAX] = jnp.transpose(turned[row].astype(F32), (1, 0))
+                wide_coupling[pl.ds(row, BLOCKS, stride=PITCH_TURN), 0:RMAX] = jnp.transpose(turned[row].astype(F32), (1, 0))
             return carry
 
         lax.fori_loop(0, RMAX // 32, body, 0)
@@ -198,7 +205,7 @@
         def body(n, carry):
             for k in range(8):
                 j = 8 * n + k
-                rows = pl.ds(pl.multiple_of(j * RMAX, RMAX), RMAX)
+                rows = pl.ds(pl.multiple_of(j * PITCH_TURN, 8), RMAX)
                 coupling[j] = wide_coupling[rows, 0:RMAX].astype(BF16)
             return carry
 
@@ -224,8 +231,8 @@
             copy_of(h, k, u, out.at[step % 4], into.at[s], near_by(axis, step)).start()
 
     def stream(p, h):
+        arrived(h, G1, 0, gathered.at[p, h, :, pl.ds(1, 3)])
         for u, (_, axis, _) in enumerate(ROUTES):
-            arrived(h, G1, u, gathered.at[p, h, u, pl.ds(1, 3)])
             plane = packed.at[p, h, u]
             packed[p, h, u, 0] = dot(compact[...], gathered[p, h, u].reshape(64, WIDE)).astype(BF16)
             for step in STEPS:
@@ -250,18 +257,18 @@
                 g = 2 * n + k
                 sides = [part[:, k * 128 : (k + 1) * 128] for part in parts]
                 for u in range(3):
-                    big_in[h, (4 * g + u) * 128 : (4 * g + u + 1) * 128, :] = sides[u]
-                big_in[h, (4 * g + 3) * 128 : (4 * g + 4) * 128, :] = fourth(sides)
+                    big_in[h, pl.ds((4 * g + u) * PITCH_BLOCK, BLOCKS), :] = sides[u]
+                big_in[h, pl.ds((4 * g + 3) * PITCH_BLOCK, BLOCKS), :] = fourth(sides)
 
         tiles(unpicks)
 
         for j in range(BLOCKS):
-            x = big_in[h, pl.ds(j, PART, stride=BLOCKS), 0:RMAX].astype(BF16)
-            big_out[h, pl.ds(j, PART, stride=BLOCKS), 0:RMAX] = dot(x, coupling[j])
-        for g in range(4):
-            extra = big_out[h, (4 * g + 3) * 128 : (4 * g + 4) * 128, :]
+            x = big_in[h, pl.ds(j, PART, stride=PITCH_BLOCK), 0:RMAX].astype(BF16)
+            big_out[h, pl.ds(j, PART, stride=PITCH_BLOCK), 0:RMAX] = dot(x, coupling[j])
+        for g in range(QUADS):
+            extra = big_out[h, pl.ds((4 * g + 3) * PITCH_BLOCK, BLOCKS), :]
             for u in range(3):
-                row = big_out[h, (4 * g + u) * 128 : (4 * g + u + 1) * 128, :]
+                row = big_out[h, pl.ds((4 * g + u) * PITCH_BLOCK, BLOCKS), :]
                 products[h, u, :, g * 128 : (g + 1) * 128] = merge(row, extra, u).astype(BF16)
         for u in range(3):
             def places(cols, n, u=u):
@@ -287,29 +294,33 @@
             for n in range(3):
                 s = s + sums_in[p, h, u, n].astype(F32)
             ends_out[p, h, u] = dot(expand[...], s.astype(BF16)).astype(BF16).reshape(4, 16, WIDE)
-            line_copies(h, R1, u, ends_out.at[p, h, u], ends_in.at[p, h, u], axis)
+            line_copies(h, R1, 0, ends_out.at[p, h, u], ends_in.at[p, h, u], axis)
         yield
         sides = []
-        for u in range(3):
-            arrived(h, R1, u, ends_in.at[p, h, u])
+        arrived(h, R1, 0, ends_in.at[p, h])
+        for u in range(3):
             s = ends_out[p, h, u, 0].astype(F32)
             for n in range(3):
                 s = s + ends_in[p, h, u, n].astype(F32)
             sides.append(s)
-        for g in range(4):
+        for g in range(QUADS):
             here = [s[:, g * 128 : (g + 1) * 128] for s in sides]
             for u in range(3):
-                small[h, (4 * g + u) * 16 : (4 * g + u + 1) * 16, :] = here[u]
-            small[h, (4 * g + 3) * 16 : (4 * g + 4) * 16, :] = fourth(here)
+                small[h, pl.ds((4 * g + u) * PITCH_CLUSTER, 16), :] = here[u]
+            small[h, pl.ds((4 * g + 3) * PITCH_CLUSTER, 16), :] = fourth(here)
         lines = pl.ds(PART * h, PART)
         masks = [mask[i : i + 1, :RMAX] for i in range(12)]
-        fields = [(small[h, pl.ds(i, PART, stride=16), 0:RMAX] * masks[i]).astype(BF16) for i in range(12)]
+        fields = [(small[h, pl.ds(i, PART, stride=PITCH_CLUSTER), 0:RMAX] * masks[i]).astype(BF16) for i in range(12)]
         downs = [dot_nt(fields[8 + i // 2], transfer[i]) for i in range(8)]
         leaves = [((fields[i].astype(F32) + downs[i]) * masks[i]).astype(BF16) for i in range(8)]
         fars = [dot(leaves[i], basis[i]) for i in range(8)]
         fars = [(near_sum[i, lines] + fars[i]).astype(BF16) for i in range(8)]
         for i in range(8):
-            v[p + 1, 1 + i, lines] = fars[i]
+            lines_of[h, i] = fars[i].astype(F32)
+        if PART * (h + 1) % 16 == 0:
+            for i in range(8):
+                parts = [lines_of[k, i] for k in range(h + 1 - 16 // PART, h + 1)]
+                v[p + 1, 1 + i, halo_rows(h)] = jnp.concatenate(parts, axis=0).astype(BF16)
 
         sent(h, G1, gathered.at[p, h, :, pl.ds(1, 3)])
         sent(h, G2, packed.at[p, h, :, pl.ds(1, 3)])
@@ -317,7 +328,8 @@
         sent(h, EX + 3, inbox.at[p, h, 1, :, pl.ds(1, 7)])
         sent(h, R2, sums_in.at[p, h])
         sent(h, R1, ends_in.at[p, h])
-        sent(h, HALO, v.at[p, pl.ds(0, 2), lines])
+        if PART * (h + 1) % 16 == 0:
+            sent(h, HALO, v.at[p, pl.ds(0, 2), halo_rows(h)])
         if p == 0:
             small[h] = jnp.zeros_like(small[h])
             coefficients(1, h)
@@ -330,8 +342,11 @@
     raw[1:2, :] = block_target[...]
     for i in range(12):
         mask[i : i + 1, :] = ones_where(iota((1, 128), 1) < ranks[0:1, i : i + 1])
+    for i in range(8):
+        whole = v[0, 1 + i].astype(F32)
+        for h in range(STREAMS):
+            lines_of[h, i] = whole[PART * h : PART * (h + 1)]
     coefficients(0, 0)
-    coefficients(0, 1)
     column, line = iota((ROWS, 64), 1), iota((ROWS, 64), 0)
     same = lax.shift_right_logical(column, 4) * 12 + (column & 15) == line
     compact[...] = ones_where(same & ((column & 15) < 12)).astype(BF16)
@@ -339,13 +354,16 @@
     same = lax.shift_right_logical(column, 4) * 12 + (column & 15) == line
     expand[...] = ones_where(same & ((column & 15) < 12)).astype(BF16)
     pl.semaphore_wait(barrier, len(peers))
-    for copy in list_copies:
-        copy.start()
-    begin(0, 0)
-    begin(0, 1)
+    for h in range(STREAMS):
+        if h > 0:
+            coefficients(0, h)
+        begin(0, h)
+        if h == 0:
+            for copy in list_copies:
+                copy.start()
 
     for p in range(2):
-        streams = [stream(p, h) for h in (0, 1)]
+        streams = [stream(p, h) for h in range(STREAMS)]
 
         def both():
             for s in streams:
@@ -390,9 +408,10 @@
             pltpu.VMEM((8, RMAX, RMAX), BF16),
             pltpu.VMEM((8, 3, LEAF, LEAF), BF16),
             pltpu.VMEM((RMAX, RMAX, BLOCKS), BF16),
-            pltpu.VMEM((BLOCKS * RMAX, 128), F32),
+            pltpu.VMEM((BLOCKS * PITCH_TURN, 128), F32),
             pltpu.VMEM((BLOCKS, RMAX, RMAX), BF16),
             pltpu.VMEM((3, 10, RHS, LEAF), BF16),
+            pltpu.VMEM((STREAMS, 8, PART, LEAF), F32),
             pltpu.VMEM((8, RHS, LEAF), F32),
             pltpu.VMEM((1, 12), jnp.int32),
             pltpu.VMEM((1, BLOCKS), jnp.int32),
@@ -404,22 +423,22 @@
             pltpu.VMEM((3, 4 * ROWS, 256), BF16),
             pltpu.VMEM((3, 128, 256), BF16),
             pltpu.VMEM((3, 256, 128), BF16),
-            pltpu.VMEM((2, PART * 16, 128), F32),
-            pltpu.VMEM((2, PART * BLOCKS, 128), F32),
-            pltpu.VMEM((2, PART * BLOCKS, 128), F32),
-            pltpu.VMEM((2, 3, BLOCKS, WIDE), BF16),
+            pltpu.VMEM((STREAMS, PART * PITCH_CLUSTER, 128), F32),
+            pltpu.VMEM((STREAMS, PART * PITCH_BLOCK, 128), F32),
+            pltpu.VMEM((STREAMS, PART * PITCH_BLOCK, 128), F32),
+            pltpu.VMEM((STREAMS, 3, BLOCKS, WIDE), BF16),
             pltpu.VMEM((ROWS, 64), BF16),
             pltpu.VMEM((64, ROWS), BF16),
-            pltpu.VMEM((2, 2, 3, 4, 16, WIDE), BF16),
-            pltpu.VMEM((2, 2, 3, 4, ROWS, WIDE), BF16),
-            pltpu.VMEM((2, 2, 2, 3, GROUPS, SLOTS, WIDE), BF16),
-            pltpu.VMEM((2, 2, 2, 3, GROUPS, SLOTS, WIDE), BF16),
-            pltpu.VMEM((2, 2, 3, 4, ROWS, WIDE), BF16),
-            pltpu.VMEM((2, 2, 3, 3, ROWS, WIDE), BF16),
-            pltpu.VMEM((2, 2, 3, 4, 16, WIDE), BF16),
-            pltpu.VMEM((2, 2, 3, 3, 16, WIDE), BF16),
-            pltpu.SemaphoreType.DMA((2, len(KINDS))),
-            pltpu.SemaphoreType.DMA((2, ARRIVALS)),
+            pltpu.VMEM((2, STREAMS, 3, 4, 16, WIDE), BF16),
+            pltpu.VMEM((2, STREAMS, 3, 4, ROWS, WIDE), BF16),
+            pltpu.VMEM((2, STREAMS, 2, 3, GROUPS, SLOTS, WIDE), BF16),
+            pltpu.VMEM((2, STREAMS, 2, 3, GROUPS, SLOTS, WIDE), BF16),
+            pltpu.VMEM((2, STREAMS, 3, 4, ROWS, WIDE), BF16),
+            pltpu.VMEM((2, STREAMS, 3, 3, ROWS, WIDE), BF16),
+            pltpu.VMEM((2, STREAMS, 3, 4, 16, WIDE), BF16),
+            pltpu.VMEM((2, STREAMS, 3, 3, 16, WIDE), BF16),
+            pltpu.SemaphoreType.DMA((STREAMS, len(KINDS))),
+            pltpu.SemaphoreType.DMA((STREAMS, ARRIVALS)),
             pltpu.SemaphoreType.DMA((3,)),
             pltpu.SemaphoreType.DMA((3,)),
             pltpu.SemaphoreType.DMA((8,)),

time: 81.5 us -> 77.7 us (0.953)
  Pallas kernels: 79 us -> 75.3 us
    pallas_call x1, Pallas kernels: 79 us -> 75.3 us  [local(): pl.pallas_call(kernel, out_shape=jax.ShapeDtypeStruct((2, 8, RHS, LEAF),...]
where the time goes in v6:
time: 77.7 us; the launch traced here: 77.6 us
  Pallas kernels  75.3 us (97%)
  local copies, waits for them, and re-layouts  1.68 us (2%)
    pallas_call x1, Pallas kernels, local(): pl.pallas_call(kernel, out_shape=jax.ShapeDtypeStruct((2, 8, RHS, LEAF),...  75.3 us
    squeeze x1, local copies, waits for them, and re-layouts, local(): return (both[0], both[1])  1.68 us

profile of v6, /device:TPU:1, one launch (start us, length us, event | category | flops | bytes accessed | tf_op | source)
XLA Modules:
  0.0 77.6 jit_solution(7450650184715145947)
XLA Ops:
  0.6 75.3 %shard_map.95 = bf16[2,8,32,256]{3,2,1,0:T(8,128)(2,1)} custom-call(bf16[8,32,256]{2,1,0:T(8,128)(2,1)} %charges_hbm.1, bf16[8,96,256]{2,1,0:T(8,128)(2,1)} %basis_hbm.1, bf16[8,96,96]{2,1,0:T(8,128)(2,1)} %transfer_hbm.1, bf16[8,3,256,256]{3,2,1,0:T(8,128)(2,1)} %near_hbm.1, bf16[96,96,128]{2,1,0:T(8,128)(2,1)} %bitcast.8, s32[1,12]{1,0:T(1,128)} %bitcast.9, ...), custom_call_target="tpu_custom_call" | custom-call | tf_op jit(solution)/shard_map/pallas_call | solution.py:401
  75.9 1.7 %slice_bitcast_fusion = (bf16[8,32,256]{2,1,0:T(8,128)(2,1)}, bf16[8,32,256]{2,1,0:T(8,128)(2,1)}) fusion(bf16[2,8,32,256]{3,2,1,0:T(8,128)(2,1)} %shard_map.95), kind=kLoop, calls=%fused_computation | loop fusion | bytes 524288 | tf_op jit(solution)/shard_map/squeeze | solution.py:451

commit v7 on v6

--- a/solution.py
+++ b/solution.py
@@ -10,7 +10,8 @@
 BF16 = jnp.bfloat16
 RMAX = 96
 RHS = 32
-STREAMS = 2
+STREAMS = 4
+TOGETHER = 2
 PART = RHS // STREAMS
 QUADS = PART // 4
 LEAF = 256
@@ -217,14 +218,16 @@
         targets = [(near_by(axis, step, o), step % 4 * 2 + o, -step % 4 * 2 + o) for step in STEPS for o in (0, 1)]
         for device, src, dst in targets + [(sibling, 1, 1)]:
             copy_of(h, EX + 3 * way, u, box.at[src], to.at[dst], device).start()
-        inbox[p, h, way, u, 0] = outbox[p, h, way, u, 0]
+
+    def fill_boxes(p, h, way, u, selector, rows):
+        for n in range(0, WIDE, 256):
+            cols = slice(n, n + 256)
+            boxes = dot(selector, rows[:, cols]).astype(BF16).reshape(GROUPS, SLOTS, 256)
+            outbox[p, h, way, u, 1:GROUPS, :, cols] = boxes[1:GROUPS]
+            inbox[p, h, way, u, 0, :, cols] = boxes[0]
 
     def exchanged(p, h, way, u):
         arrived(h, EX + 3 * way, u, inbox.at[p, h, way, u, pl.ds(1, 7)])
-
-    def tiles(body):
-        for n in range(WIDE // 256):
-            body(slice(256 * n, 256 * n + 256), n)
 
     def line_copies(h, k, u, out, into, axis):
         for s, step in enumerate(STEPS):
@@ -232,68 +235,65 @@
 
     def stream(p, h):
         arrived(h, G1, 0, gathered.at[p, h, :, pl.ds(1, 3)])
+        for u in range(3):
+            packed[p, h, u, 0] = dot(compact[...], gathered[p, h, u].reshape(64, WIDE)).astype(BF16)
         for u, (_, axis, _) in enumerate(ROUTES):
             plane = packed.at[p, h, u]
-            packed[p, h, u, 0] = dot(compact[...], gathered[p, h, u].reshape(64, WIDE)).astype(BF16)
             for step in STEPS:
                 copy_of(h, G2, u, plane.at[0], plane.at[-step % 4], near_by(axis, step)).start()
         yield
         for u in range(3):
             arrived(h, G2, u, packed.at[p, h, u, pl.ds(1, 3)])
-
-            def picks(cols, n, u=u):
-                rows = packed[p, h, u, :, :, cols].reshape(4 * ROWS, 256)
-                outbox[p, h, 0, u, :, :, cols] = dot(pick[u], rows).astype(BF16).reshape(GROUPS, SLOTS, 256)
-
-            tiles(picks)
+        for u in range(3):
+            fill_boxes(p, h, 0, u, pick[u], packed[p, h, u].reshape(4 * ROWS, WIDE))
+        for u in range(3):
             exchange(p, h, 0, u)
         yield
+        batch, first_row = h // TOGETHER, PART * (h % TOGETHER)
         for u in range(3):
             exchanged(p, h, 0, u)
 
-        def unpicks(cols, n):
-            parts = [dot(unpick[u], inbox[p, h, 0, u, :, :, cols].reshape(256, 256)) for u in range(3)]
+        for n in range(0, WIDE, 256):
+            parts = [dot(unpick[u], inbox[p, h, 0, u, :, :, n : n + 256].reshape(256, 256)) for u in range(3)]
             for k in range(2):
-                g = 2 * n + k
+                g = n // 128 + k
                 sides = [part[:, k * 128 : (k + 1) * 128] for part in parts]
+                for k, side in enumerate(sides + [fourth(sides)]):
+                    big_in[batch, pl.ds((first_row + 4 * g + k) * PITCH_BLOCK, BLOCKS), :] = side
+
+        if (h + 1) % TOGETHER == 0:
+            lines_at_once = PART * TOGETHER
+            for j in range(BLOCKS):
+                x = big_in[batch, pl.ds(j, lines_at_once, stride=PITCH_BLOCK), 0:RMAX].astype(BF16)
+                big_out[batch, pl.ds(j, lines_at_once, stride=PITCH_BLOCK), 0:RMAX] = dot(x, coupling[j])
+            for k in range(h + 1 - TOGETHER, h + 1):
+                for g in range(QUADS):
+                    row = PART * (k % TOGETHER) + 4 * g
+                    parts = [big_out[batch, pl.ds((row + u) * PITCH_BLOCK, BLOCKS), :] for u in range(4)]
+                    for u in range(3):
+                        products[k, u, :, g * 128 : (g + 1) * 128] = merge(parts[u], parts[3], u).astype(BF16)
                 for u in range(3):
-                    big_in[h, pl.ds((4 * g + u) * PITCH_BLOCK, BLOCKS), :] = sides[u]
-                big_in[h, pl.ds((4 * g + 3) * PITCH_BLOCK, BLOCKS), :] = fourth(sides)
-
-        tiles(unpicks)
-
-        for j in range(BLOCKS):
-            x = big_in[h, pl.ds(j, PART, stride=PITCH_BLOCK), 0:RMAX].astype(BF16)
-            big_out[h, pl.ds(j, PART, stride=PITCH_BLOCK), 0:RMAX] = dot(x, coupling[j])
-        for g in range(QUADS):
-            extra = big_out[h, pl.ds((4 * g + 3) * PITCH_BLOCK, BLOCKS), :]
-            for u in range(3):
-                row = big_out[h, pl.ds((4 * g + u) * PITCH_BLOCK, BLOCKS), :]
-                products[h, u, :, g * 128 : (g + 1) * 128] = merge(row, extra, u).astype(BF16)
-        for u in range(3):
-            def places(cols, n, u=u):
-                terms = dot(place[u], products[h, u, :, cols]).astype(BF16)
-                outbox[p, h, 1, u, :, :, cols] = terms.reshape(GROUPS, SLOTS, 256)
-
-            tiles(places)
-            exchange(p, h, 1, u)
-        yield
+                    fill_boxes(p, k, 1, u, place[u], products[k, u])
+                for u in range(3):
+                    exchange(p, k, 1, u)
+        yield
+        for u in range(3):
+            exchanged(p, h, 1, u)
+        for u in range(3):
+            for n in range(0, WIDE, 256):
+                rows = inbox[p, h, 1, u, :, :, n : n + 256].reshape(256, 256)
+                sums_out[p, h, u, :, :, n : n + 256] = dot(scatter[u], rows).astype(BF16).reshape(4, ROWS, 256)
         for u, (_, axis, _) in enumerate(ROUTES):
-            exchanged(p, h, 1, u)
-
-            def sums(cols, n, u=u):
-                rows = inbox[p, h, 1, u, :, :, cols].reshape(256, 256)
-                sums_out[p, h, u, :, :, cols] = dot(scatter[u], rows).astype(BF16).reshape(4, ROWS, 256)
-
-            tiles(sums)
             line_copies(h, R2, u, sums_out.at[p, h, u], sums_in.at[p, h, u], axis)
         yield
-        for u, (axis, _, _) in enumerate(ROUTES):
+        for u in range(3):
             arrived(h, R2, u, sums_in.at[p, h, u])
+        for u in range(3):
             s = sums_out[p, h, u, 0].astype(F32)
             for n in range(3):
                 s = s + sums_in[p, h, u, n].astype(F32)
             ends_out[p, h, u] = dot(expand[...], s.astype(BF16)).astype(BF16).reshape(4, 16, WIDE)
+        for u, (axis, _, _) in enumerate(ROUTES):
             line_copies(h, R1, 0, ends_out.at[p, h, u], ends_in.at[p, h, u], axis)
         yield
         sides = []
@@ -424,8 +424,8 @@
             pltpu.VMEM((3, 128, 256), BF16),
             pltpu.VMEM((3, 256, 128), BF16),
             pltpu.VMEM((STREAMS, PART * PITCH_CLUSTER, 128), F32),
-            pltpu.VMEM((STREAMS, PART * PITCH_BLOCK, 128), F32),
-            pltpu.VMEM((STREAMS, PART * PITCH_BLOCK, 128), F32),
+            pltpu.VMEM((STREAMS // TOGETHER, PART * TOGETHER * PITCH_BLOCK, 128), F32),
+            pltpu.VMEM((STREAMS // TOGETHER, PART * TOGETHER * PITCH_BLOCK, 128), F32),
             pltpu.VMEM((STREAMS, 3, BLOCKS, WIDE), BF16),
             pltpu.VMEM((ROWS, 64), BF16),
             pltpu.VMEM((64, ROWS), BF16),

time: 77.7 us -> 74.9 us (0.964)
  Pallas kernels: 75.3 us -> 72.5 us
    pallas_call x1, Pallas kernels: 75.3 us -> 72.5 us  [local(): pl.pallas_call(kernel, out_shape=jax.ShapeDtypeStruct((2, 8, RHS, LEAF),...]
where the time goes in v7:
time: 74.9 us; the launch traced here: 74.8 us
  Pallas kernels  72.5 us (97%)
  local copies, waits for them, and re-layouts  1.68 us (2%)
    pallas_call x1, Pallas kernels, local(): pl.pallas_call(kernel, out_shape=jax.ShapeDtypeStruct((2, 8, RHS, LEAF),...  72.5 us
    squeeze x1, local copies, waits for them, and re-layouts, local(): return (both[0], both[1])  1.68 us

profile of v7, /device:TPU:1, one launch (start us, length us, event | category | flops | bytes accessed | tf_op | source)
XLA Modules:
  0.0 74.8 jit_solution(17391608844056821427)
XLA Ops:
  0.6 72.5 %shard_map.95 = bf16[2,8,32,256]{3,2,1,0:T(8,128)(2,1)} custom-call(bf16[8,32,256]{2,1,0:T(8,128)(2,1)} %charges_hbm.1, bf16[8,96,256]{2,1,0:T(8,128)(2,1)} %basis_hbm.1, bf16[8,96,96]{2,1,0:T(8,128)(2,1)} %transfer_hbm.1, bf16[8,3,256,256]{3,2,1,0:T(8,128)(2,1)} %near_hbm.1, bf16[96,96,128]{2,1,0:T(8,128)(2,1)} %bitcast.8, s32[1,12]{1,0:T(1,128)} %bitcast.9, ...), custom_call_target="tpu_custom_call" | custom-call | tf_op jit(solution)/shard_map/pallas_call | solution.py:401
  73.1 1.7 %slice_bitcast_fusion = (bf16[8,32,256]{2,1,0:T(8,128)(2,1)}, bf16[8,32,256]{2,1,0:T(8,128)(2,1)}) fusion(bf16[2,8,32,256]{3,2,1,0:T(8,128)(2,1)} %shard_map.95), kind=kLoop, calls=%fused_computation | loop fusion | bytes 524288 | tf_op jit(solution)/shard_map/squeeze | solution.py:451

commit v8 on v7

--- a/solution.py
+++ b/solution.py
@@ -23,9 +23,7 @@
 SLOTS = 32
 BLOCKS = 128
 
-G1, G2, EX, R2, R1, HALO = 0, 1, 4, 10, 13, 14
-ARRIVALS = 15
-KINDS = {G1: 0, G2: 1, EX: 2, EX + 3: 3, R2: 4, R1: 5, HALO: 6}
+G1, G2, EX, BACK, R2, R1, HALO = range(7)
 ROWS = 48
 PITCH_BLOCK, PITCH_CLUSTER, PITCH_TURN = 136, 24, 104
 
@@ -95,30 +93,34 @@
     small[...] = jnp.zeros_like(small)
     raw[...] = jnp.zeros_like(raw)
 
-    def copy_of(h, k, u, src, dst, device):
+    def copy_of(h, k, src, dst, device):
         return pltpu.make_async_remote_copy(
-            src_ref=src, dst_ref=dst, send_sem=send_sem.at[h, KINDS[k]], recv_sem=recv_sem.at[h, k + u],
+            src_ref=src, dst_ref=dst, send_sem=send_sem.at[k], recv_sem=recv_sem.at[h, k],
             device_id=(device,), device_id_type=MESH)
 
-    def arrived(h, k, u, where):
-        copy_of(h, k, u, where, where, sibling).wait_recv()
-
-    def sent(h, k, where):
-        copy_of(h, k, 0, where, where, sibling).wait_send()
-
-    def coefficients(p, h):
+    def arrived(h, k, where):
+        copy_of(h, k, where, where, sibling).wait_recv()
+
+    def sent(k, where):
+        copy_of(0, k, where, where, sibling).wait_send()
+
+    def coefficients(p, streams):
         masks = [mask[i : i + 1, :RMAX] for i in range(12)]
-        leaves = [dot_nt(lines_of[h, i].astype(BF16), basis[i]) for i in range(8)]
+        fields = [jnp.concatenate([lines_of[h, i] for h in streams], axis=0).astype(BF16) for i in range(8)]
+        leaves = [dot_nt(fields[i], basis[i]) for i in range(8)]
         leaves = [(c * m).astype(BF16) for c, m in zip(leaves, masks)]
         lifted = [dot(c, transfer[i]) for i, c in enumerate(leaves)]
         above = [((lifted[2 * q] + lifted[2 * q + 1]) * masks[8 + q]).astype(BF16) for q in range(4)]
         for i, c in enumerate(leaves + above):
-            small[h, pl.ds(i, PART, stride=PITCH_CLUSTER), 0:RMAX] = c.astype(F32)
-        for u in range(3):
-            for g in range(QUADS):
-                row = small[h, pl.ds((4 * g + u) * PITCH_CLUSTER, 16), :]
-                extra = small[h, pl.ds((4 * g + 3) * PITCH_CLUSTER, 16), :]
-                gathered[p, h, u, 0, :, g * 128 : (g + 1) * 128] = merge(row, extra, u).astype(BF16)
+            c = c.astype(F32)
+            for k, h in enumerate(streams):
+                small[h, pl.ds(i, PART, stride=PITCH_CLUSTER), 0:RMAX] = c[PART * k : PART * (k + 1)]
+        for h in streams:
+            for u in range(3):
+                for g in range(QUADS):
+                    row = small[h, pl.ds((4 * g + u) * PITCH_CLUSTER, 16), :]
+                    extra = small[h, pl.ds((4 * g + 3) * PITCH_CLUSTER, 16), :]
+                    gathered[p, h, u, 0, :, g * 128 : (g + 1) * 128] = merge(row, extra, u).astype(BF16)
 
     def halo_rows(h):
         return pl.ds(16 * (PART * h // 16), 16)
@@ -127,17 +129,17 @@
         for u, (axis, _, _) in enumerate(ROUTES):
             block = gathered.at[p, h, u]
             for step in STEPS:
-                copy_of(h, G1, 0, block.at[0], block.at[-step % 4], near_by(axis, step)).start()
+                copy_of(h, G1, block.at[0], block.at[-step % 4], near_by(axis, step)).start()
         if PART * (h + 1) % 16 == 0:
             rows = halo_rows(h)
-            copy_of(h, HALO, 0, v.at[p, 1, rows], v.at[p, 9, rows], before).start()
-            copy_of(h, HALO, 0, v.at[p, 8, rows], v.at[p, 0, rows], after).start()
+            copy_of(h, HALO, v.at[p, 1, rows], v.at[p, 9, rows], before).start()
+            copy_of(h, HALO, v.at[p, 8, rows], v.at[p, 0, rows], after).start()
 
     def near_part(p, lo, hi):
         if lo == 0:
             for h in range(STREAMS):
                 if PART * (h + 1) % 16 == 0:
-                    arrived(h, HALO, 0, v.at[p, pl.ds(0, 2), halo_rows(h)])
+                    arrived(h, HALO, v.at[p, pl.ds(0, 2), halo_rows(h)])
             v[p, 0] = (v[p, 0].astype(F32) * (me > 0).astype(F32)).astype(BF16)
             v[p, 9] = (v[p, 9].astype(F32) * (me < devices - 1).astype(F32)).astype(BF16)
         for i in range(lo, hi):
@@ -151,7 +153,7 @@
         for device, group in targets:
             list_copies.append(pltpu.make_async_remote_copy(
                 src_ref=raw, dst_ref=raw_in.at[u, pl.ds(8 * group, 8)],
-                send_sem=list_send.at[u], recv_sem=list_recv.at[u],
+                send_sem=list_send.at[0], recv_sem=list_recv.at[0],
                 device_id=(device,), device_id_type=MESH))
 
     def place_of(ids, route):
@@ -180,7 +182,7 @@
             raw_in[u, 0:8, :] = raw[...]
             pick[u] = rows_wanted(u, 0).astype(BF16)
 
-    def make_others():
+    def make_own():
         number = iota((256, 128), 0).astype(F32)
         for u, route in enumerate(ROUTES):
             group, _ = place_of(raw[...], route)
@@ -191,6 +193,9 @@
                 slots.append(group[k : k + 1, :].astype(F32) * SLOTS + rank)
             unpick[u] = jnp.transpose(ones_where(number == slots[0]), (1, 0)).astype(BF16)
             place[u] = ones_where(number == slots[1]).astype(BF16)
+
+    def make_sums():
+        for u in range(3):
             scatter[u] = jnp.transpose(rows_wanted(u, 1), (1, 0)).astype(BF16)
 
     def turn():
@@ -217,7 +222,7 @@
         box, to = outbox.at[p, h, way, u], inbox.at[p, h, way, u]
         targets = [(near_by(axis, step, o), step % 4 * 2 + o, -step % 4 * 2 + o) for step in STEPS for o in (0, 1)]
         for device, src, dst in targets + [(sibling, 1, 1)]:
-            copy_of(h, EX + 3 * way, u, box.at[src], to.at[dst], device).start()
+            copy_of(h, BACK if way else EX, box.at[src], to.at[dst], device).start()
 
     def fill_boxes(p, h, way, u, selector, rows):
         for n in range(0, WIDE, 256):
@@ -226,32 +231,30 @@
             outbox[p, h, way, u, 1:GROUPS, :, cols] = boxes[1:GROUPS]
             inbox[p, h, way, u, 0, :, cols] = boxes[0]
 
-    def exchanged(p, h, way, u):
-        arrived(h, EX + 3 * way, u, inbox.at[p, h, way, u, pl.ds(1, 7)])
-
-    def line_copies(h, k, u, out, into, axis):
+    def exchanged(p, h, way):
+        arrived(h, BACK if way else EX, inbox.at[p, h, way, :, pl.ds(1, 7)])
+
+    def line_copies(h, k, out, into, axis):
         for s, step in enumerate(STEPS):
-            copy_of(h, k, u, out.at[step % 4], into.at[s], near_by(axis, step)).start()
+            copy_of(h, k, out.at[step % 4], into.at[s], near_by(axis, step)).start()
 
     def stream(p, h):
-        arrived(h, G1, 0, gathered.at[p, h, :, pl.ds(1, 3)])
+        arrived(h, G1, gathered.at[p, h, :, pl.ds(1, 3)])
         for u in range(3):
             packed[p, h, u, 0] = dot(compact[...], gathered[p, h, u].reshape(64, WIDE)).astype(BF16)
         for u, (_, axis, _) in enumerate(ROUTES):
             plane = packed.at[p, h, u]
             for step in STEPS:
-                copy_of(h, G2, u, plane.at[0], plane.at[-step % 4], near_by(axis, step)).start()
-        yield
-        for u in range(3):
-            arrived(h, G2, u, packed.at[p, h, u, pl.ds(1, 3)])
+                copy_of(h, G2, plane.at[0], plane.at[-step % 4], near_by(axis, step)).start()
+        yield
+        arrived(h, G2, packed.at[p, h, :, pl.ds(1, 3)])
         for u in range(3):
             fill_boxes(p, h, 0, u, pick[u], packed[p, h, u].reshape(4 * ROWS, WIDE))
         for u in range(3):
             exchange(p, h, 0, u)
         yield
         batch, first_row = h // TOGETHER, PART * (h % TOGETHER)
-        for u in range(3):
-            exchanged(p, h, 0, u)
+        exchanged(p, h, 0)
 
         for n in range(0, WIDE, 256):
             parts = [dot(unpick[u], inbox[p, h, 0, u, :, :, n : n + 256].reshape(256, 256)) for u in range(3)]
@@ -277,27 +280,25 @@
                 for u in range(3):
                     exchange(p, k, 1, u)
         yield
-        for u in range(3):
-            exchanged(p, h, 1, u)
+        exchanged(p, h, 1)
         for u in range(3):
             for n in range(0, WIDE, 256):
                 rows = inbox[p, h, 1, u, :, :, n : n + 256].reshape(256, 256)
                 sums_out[p, h, u, :, :, n : n + 256] = dot(scatter[u], rows).astype(BF16).reshape(4, ROWS, 256)
         for u, (_, axis, _) in enumerate(ROUTES):
-            line_copies(h, R2, u, sums_out.at[p, h, u], sums_in.at[p, h, u], axis)
-        yield
-        for u in range(3):
-            arrived(h, R2, u, sums_in.at[p, h, u])
+            line_copies(h, R2, sums_out.at[p, h, u], sums_in.at[p, h, u], axis)
+        yield
+        arrived(h, R2, sums_in.at[p, h])
         for u in range(3):
             s = sums_out[p, h, u, 0].astype(F32)
             for n in range(3):
                 s = s + sums_in[p, h, u, n].astype(F32)
             ends_out[p, h, u] = dot(expand[...], s.astype(BF16)).astype(BF16).reshape(4, 16, WIDE)
         for u, (axis, _, _) in enumerate(ROUTES):
-            line_copies(h, R1, 0, ends_out.at[p, h, u], ends_in.at[p, h, u], axis)
+            line_copies(h, R1, ends_out.at[p, h, u], ends_in.at[p, h, u], axis)
         yield
         sides = []
-        arrived(h, R1, 0, ends_in.at[p, h])
+        arrived(h, R1, ends_in.at[p, h])
         for u in range(3):
             s = ends_out[p, h, u, 0].astype(F32)
             for n in range(3):
@@ -322,17 +323,8 @@
                 parts = [lines_of[k, i] for k in range(h + 1 - 16 // PART, h + 1)]
                 v[p + 1, 1 + i, halo_rows(h)] = jnp.concatenate(parts, axis=0).astype(BF16)
 
-        sent(h, G1, gathered.at[p, h, :, pl.ds(1, 3)])
-        sent(h, G2, packed.at[p, h, :, pl.ds(1, 3)])
-        sent(h, EX, inbox.at[p, h, 0, :, pl.ds(1, 7)])
-        sent(h, EX + 3, inbox.at[p, h, 1, :, pl.ds(1, 7)])
-        sent(h, R2, sums_in.at[p, h])
-        sent(h, R1, ends_in.at[p, h])
-        if PART * (h + 1) % 16 == 0:
-            sent(h, HALO, v.at[p, pl.ds(0, 2), halo_rows(h)])
         if p == 0:
-            small[h] = jnp.zeros_like(small[h])
-            coefficients(1, h)
+            coefficients(1, [h])
             begin(1, h)
         yield
 
@@ -346,7 +338,7 @@
         whole = v[0, 1 + i].astype(F32)
         for h in range(STREAMS):
             lines_of[h, i] = whole[PART * h : PART * (h + 1)]
-    coefficients(0, 0)
+    coefficients(0, range(STREAMS))
     column, line = iota((ROWS, 64), 1), iota((ROWS, 64), 0)
     same = lax.shift_right_logical(column, 4) * 12 + (column & 15) == line
     compact[...] = ones_where(same & ((column & 15) < 12)).astype(BF16)
@@ -355,12 +347,12 @@
     expand[...] = ones_where(same & ((column & 15) < 12)).astype(BF16)
     pl.semaphore_wait(barrier, len(peers))
     for h in range(STREAMS):
-        if h > 0:
-            coefficients(0, h)
         begin(0, h)
-        if h == 0:
-            for copy in list_copies:
-                copy.start()
+    for copy in list_copies:
+        copy.start()
+    make_own()
+    load_coupling.wait()
+    turn()
 
     for p in range(2):
         streams = [stream(p, h) for h in range(STREAMS)]
@@ -371,19 +363,16 @@
 
         both()
         if p == 0:
-            for u in range(3):
-                tiles_in = raw_in.at[u, pl.ds(8, 56)]
-                pltpu.make_async_remote_copy(
-                    src_ref=tiles_in, dst_ref=tiles_in, send_sem=list_send.at[u], recv_sem=list_recv.at[u],
-                    device_id=(sibling,), device_id_type=MESH).wait()
+            tiles_in = raw_in.at[:, pl.ds(8, 56)]
+            pltpu.make_async_remote_copy(
+                src_ref=tiles_in, dst_ref=tiles_in, send_sem=list_send.at[0], recv_sem=list_recv.at[0],
+                device_id=(sibling,), device_id_type=MESH).wait()
             make_picks()
         else:
             near_part(p, 0, 4)
         both()
         if p == 0:
-            make_others()
-            load_coupling.wait()
-            turn()
+            make_sums()
             narrow()
             load_near.wait()
             near_part(p, 0, 4)
@@ -393,6 +382,13 @@
         both()
         both()
     out[...] = v[1:3, 1:9]
+    sent(G1, gathered.at[:, :, :, pl.ds(1, 3)])
+    sent(G2, packed.at[:, :, :, pl.ds(1, 3)])
+    sent(EX, inbox.at[:, :, 0, :, pl.ds(1, 7)])
+    sent(BACK, inbox.at[:, :, 1, :, pl.ds(1, 7)])
+    sent(R2, sums_in)
+    sent(R1, ends_in)
+    sent(HALO, v.at[0, pl.ds(0, 4)])
 
 
 def local(charges, basis, transfer, near_field, coupling, ranks, block_source, block_target):
@@ -437,10 +433,10 @@
             pltpu.VMEM((2, STREAMS, 3, 3, ROWS, WIDE), BF16),
             pltpu.VMEM((2, STREAMS, 3, 4, 16, WIDE), BF16),
             pltpu.VMEM((2, STREAMS, 3, 3, 16, WIDE), BF16),
-            pltpu.SemaphoreType.DMA((STREAMS, len(KINDS))),
-            pltpu.SemaphoreType.DMA((STREAMS, ARRIVALS)),
-            pltpu.SemaphoreType.DMA((3,)),
-            pltpu.SemaphoreType.DMA((3,)),
+            pltpu.SemaphoreType.DMA((HALO + 1,)),
+            pltpu.SemaphoreType.DMA((STREAMS, HALO + 1)),
+            pltpu.SemaphoreType.DMA((1,)),
+            pltpu.SemaphoreType.DMA((1,)),
             pltpu.SemaphoreType.DMA((8,)),
         ],
         compiler_params=pltpu.CompilerParams(

time: 74.9 us -> 73.2 us (0.977)
  Pallas kernels: 72.5 us -> 70.7 us
    pallas_call x1, Pallas kernels: 72.5 us -> 70.7 us  [local(): pl.pallas_call(kernel, out_shape=jax.ShapeDtypeStruct((2, 8, RHS, LEAF),...]
where the time goes in v8:
time: 73.2 us; the launch traced here: 73.1 us
  Pallas kernels  70.7 us (97%)
  local copies, waits for them, and re-layouts  1.68 us (2%)
    pallas_call x1, Pallas kernels, local(): pl.pallas_call(kernel, out_shape=jax.ShapeDtypeStruct((2, 8, RHS, LEAF),...  70.7 us
    squeeze x1, local copies, waits for them, and re-layouts, local(): return (both[0], both[1])  1.68 us

profile of v8, /device:TPU:1, one launch (start us, length us, event | category | flops | bytes accessed | tf_op | source)
XLA Modules:
  0.0 73.1 jit_solution(11179154314005508435)
XLA Ops:
  0.6 70.7 %shard_map.95 = bf16[2,8,32,256]{3,2,1,0:T(8,128)(2,1)} custom-call(bf16[8,32,256]{2,1,0:T(8,128)(2,1)} %charges_hbm.1, bf16[8,96,256]{2,1,0:T(8,128)(2,1)} %basis_hbm.1, bf16[8,96,96]{2,1,0:T(8,128)(2,1)} %transfer_hbm.1, bf16[8,3,256,256]{3,2,1,0:T(8,128)(2,1)} %near_hbm.1, bf16[96,96,128]{2,1,0:T(8,128)(2,1)} %bitcast.8, s32[1,12]{1,0:T(1,128)} %bitcast.9, ...), custom_call_target="tpu_custom_call" | custom-call | tf_op jit(solution)/shard_map/pallas_call | solution.py:397
  71.4 1.7 %slice_bitcast_fusion = (bf16[8,32,256]{2,1,0:T(8,128)(2,1)}, bf16[8,32,256]{2,1,0:T(8,128)(2,1)}) fusion(bf16[2,8,32,256]{3,2,1,0:T(8,128)(2,1)} %shard_map.95), kind=kLoop, calls=%fused_computation | loop fusion | bytes 524288 | tf_op jit(solution)/shard_map/squeeze | solution.py:447

commit v9 on v8

--- a/solution.py
+++ b/solution.py
@@ -404,7 +404,7 @@
             pltpu.VMEM((8, RMAX, RMAX), BF16),
             pltpu.VMEM((8, 3, LEAF, LEAF), BF16),
             pltpu.VMEM((RMAX, RMAX, BLOCKS), BF16),
-            pltpu.VMEM((BLOCKS * PITCH_TURN, 128), F32),
+            pltpu.VMEM(((BLOCKS + 1) * PITCH_TURN, 128), F32),
             pltpu.VMEM((BLOCKS, RMAX, RMAX), BF16),
             pltpu.VMEM((3, 10, RHS, LEAF), BF16),
             pltpu.VMEM((STREAMS, 8, PART, LEAF), F32),
@@ -414,14 +414,14 @@
             pltpu.VMEM((1, BLOCKS), jnp.int32),
             pltpu.VMEM((16, 128), F32),
             pltpu.VMEM((8, 128), jnp.int32),
-            pltpu.VMEM((3, 64, 128), jnp.int32),
+            pltpu.VMEM((3, 72, 128), jnp.int32),
             pltpu.VMEM((3, 256, 4 * ROWS), BF16),
             pltpu.VMEM((3, 4 * ROWS, 256), BF16),
             pltpu.VMEM((3, 128, 256), BF16),
             pltpu.VMEM((3, 256, 128), BF16),
-            pltpu.VMEM((STREAMS, PART * PITCH_CLUSTER, 128), F32),
-            pltpu.VMEM((STREAMS // TOGETHER, PART * TOGETHER * PITCH_BLOCK, 128), F32),
-            pltpu.VMEM((STREAMS // TOGETHER, PART * TOGETHER * PITCH_BLOCK, 128), F32),
+            pltpu.VMEM((STREAMS, (PART + 1) * PITCH_CLUSTER, 128), F32),
+            pltpu.VMEM((STREAMS // TOGETHER, (PART * TOGETHER + 1) * PITCH_BLOCK, 128), F32),
+            pltpu.VMEM((STREAMS // TOGETHER, (PART * TOGETHER + 1) * PITCH_BLOCK, 128), F32),
             pltpu.VMEM((STREAMS, 3, BLOCKS, WIDE), BF16),
             pltpu.VMEM((ROWS, 64), BF16),
             pltpu.VMEM((64, ROWS), BF16),

time: 73.2 us -> 73.2 us (level)
  no operation moved by 1% of the time
where the time goes in v9:
time: 73.2 us; the launch traced here: 73.1 us
  Pallas kernels  70.7 us (97%)
  local copies, waits for them, and re-layouts  1.68 us (2%)
    pallas_call x1, Pallas kernels, local(): pl.pallas_call(kernel, out_shape=jax.ShapeDtypeStruct((2, 8, RHS, LEAF),...  70.7 us
    squeeze x1, local copies, waits for them, and re-layouts, local(): return (both[0], both[1])  1.68 us

profile of v9, /device:TPU:1, one launch (start us, length us, event | category | flops | bytes accessed | tf_op | source)
XLA Modules:
  0.0 73.1 jit_solution(384946932440852955)
XLA Ops:
  0.6 70.7 %shard_map.95 = bf16[2,8,32,256]{3,2,1,0:T(8,128)(2,1)} custom-call(bf16[8,32,256]{2,1,0:T(8,128)(2,1)} %charges_hbm.1, bf16[8,96,256]{2,1,0:T(8,128)(2,1)} %basis_hbm.1, bf16[8,96,96]{2,1,0:T(8,128)(2,1)} %transfer_hbm.1, bf16[8,3,256,256]{3,2,1,0:T(8,128)(2,1)} %near_hbm.1, bf16[96,96,128]{2,1,0:T(8,128)(2,1)} %bitcast.8, s32[1,12]{1,0:T(1,128)} %bitcast.9, ...), custom_call_target="tpu_custom_call" | custom-call | tf_op jit(solution)/shard_map/pallas_call | solution.py:397
  71.4 1.7 %slice_bitcast_fusion = (bf16[8,32,256]{2,1,0:T(8,128)(2,1)}, bf16[8,32,256]{2,1,0:T(8,128)(2,1)}) fusion(bf16[2,8,32,256]{3,2,1,0:T(8,128)(2,1)} %shard_map.95), kind=kLoop, calls=%fused_computation | loop fusion | bytes 524288 | tf_op jit(solution)/shard_map/squeeze | solution.py:447

commit v10 on v9

--- a/solution.py
+++ b/solution.py
@@ -353,6 +353,8 @@
     make_own()
     load_coupling.wait()
     turn()
+    narrow()
+    load_near.wait()
 
     for p in range(2):
         streams = [stream(p, h) for h in range(STREAMS)]
@@ -368,14 +370,10 @@
                 src_ref=tiles_in, dst_ref=tiles_in, send_sem=list_send.at[0], recv_sem=list_recv.at[0],
                 device_id=(sibling,), device_id_type=MESH).wait()
             make_picks()
-        else:
-            near_part(p, 0, 4)
+        near_part(p, 0, 4)
         both()
         if p == 0:
             make_sums()
-            narrow()
-            load_near.wait()
-            near_part(p, 0, 4)
         near_part(p, 4, 8)
         both()
         both()

time: 73.2 us -> 73.4 us (level)
  no operation moved by 1% of the time
where the time goes in v10:
time: 73.4 us; the launch traced here: 73.3 us
  Pallas kernels  71 us (97%)
  local copies, waits for them, and re-layouts  1.68 us (2%)
    pallas_call x1, Pallas kernels, local(): pl.pallas_call(kernel, out_shape=jax.ShapeDtypeStruct((2, 8, RHS, LEAF),...  71 us
    squeeze x1, local copies, waits for them, and re-layouts, local(): return (both[0], both[1])  1.68 us

profile of v10, /device:TPU:1, one launch (start us, length us, event | category | flops | bytes accessed | tf_op | source)
XLA Modules:
  0.0 73.3 jit_solution(10234921843811369854)
XLA Ops:
  0.6 71.0 %shard_map.95 = bf16[2,8,32,256]{3,2,1,0:T(8,128)(2,1)} custom-call(bf16[8,32,256]{2,1,0:T(8,128)(2,1)} %charges_hbm.1, bf16[8,96,256]{2,1,0:T(8,128)(2,1)} %basis_hbm.1, bf16[8,96,96]{2,1,0:T(8,128)(2,1)} %transfer_hbm.1, bf16[8,3,256,256]{3,2,1,0:T(8,128)(2,1)} %near_hbm.1, bf16[96,96,128]{2,1,0:T(8,128)(2,1)} %bitcast.8, s32[1,12]{1,0:T(1,128)} %bitcast.9, ...), custom_call_target="tpu_custom_call" | custom-call | tf_op jit(solution)/shard_map/pallas_call | solution.py:395
  71.6 1.7 %slice_bitcast_fusion = (bf16[8,32,256]{2,1,0:T(8,128)(2,1)}, bf16[8,32,256]{2,1,0:T(8,128)(2,1)}) fusion(bf16[2,8,32,256]{3,2,1,0:T(8,128)(2,1)} %shard_map.95), kind=kLoop, calls=%fused_computation | loop fusion | bytes 524288 | tf_op jit(solution)/shard_map/squeeze | solution.py:445
